TPU v7x, 32 devices: a whole 2x2x4 slice. The times are simulated.
32 devices in a mesh: heads: 4 (over z), batch: 8 (over y, x, core).
Axes of the slice: x: 2, y: 2, z: 4, core: 2. Of those that a mesh axis runs over, the one named last changes fastest.
Arguments:
- student_rows: bfloat16 [32, 1024, 384], P(('batch', 'heads')), may hold values from -6 to 6
- teacher_rows: bfloat16 [32, 1024, 768], P(('batch', 'heads')), may hold values from -6 to 6
- valid_length: int32 [32], P('batch'), may hold values from 512 to 1024, as said below
- split_point: int32 [32], P('batch'), may hold values from 2 to 1022, as said below
- project_five: bfloat16 [384, 3, 384], P(None, None, 'heads'), may hold values from -0.3125 to 0.3125
- bias_five: bfloat16 [2, 384], P(None, 'heads'), may hold values from -3 to 3
- output_five: bfloat16 [384, 384], P('heads'), may hold values from -1.25 to 1.25
- branch_bias: float32 [2, 384], replicated, may hold values from -2 to 2
- norm_gain: float32 [2, 384], replicated, may hold values from 0.5 to 1.5
- norm_bias: float32 [2, 384], replicated, may hold values from -2 to 2
- widen_weight: bfloat16 [384, 1536], P(None, 'heads'), may hold values from -0.3125 to 0.3125
- widen_bias: bfloat16 [1536], P('heads'), may hold values from -3 to 3
- narrow_weight: bfloat16 [1536, 384], P('heads'), may hold values from -0.15625 to 0.15625
- project_six: bfloat16 [384, 3, 384], P(None, None, 'heads'), may hold values from -0.3125 to 0.3125
- bias_six: bfloat16 [2, 384], P(None, 'heads'), may hold values from -3 to 3
- teacher_project: bfloat16 [768, 3, 768], P(None, None, 'heads'), may hold values from -0.21875 to 0.21875
- teacher_bias: bfloat16 [2, 768], P(None, 'heads'), may hold values from -3 to 3
Outputs:
- block_out: bfloat16 [32, 1024, 384], P(('batch', 'heads'))
- grad_in: float32 [32, 1024, 384], P(('batch', 'heads'))
- grad_project_five: float32 [384, 3, 384], P(None, None, 'heads')
- grad_bias_five: float32 [2, 384], P(None, 'heads')
- grad_output_five: float32 [384, 384], P('heads')
- grad_branch_bias: float32 [2, 384], replicated
- grad_norm_gain: float32 [2, 384], replicated
- grad_norm_bias: float32 [2, 384], replicated
- grad_widen_weight: float32 [384, 1536], P(None, 'heads')
- grad_widen_bias: float32 [1536], P('heads')
- grad_narrow_weight: float32 [1536, 384], P('heads')
- grad_project_six: float32 [384, 3, 384], P(None, None, 'heads')
- grad_bias_six: float32 [2, 384], P(None, 'heads')
- summary: float32 [4], replicated
Inputs may be any that keep to these rules, and one draw needn't show every extreme that they name: `valid_length`: in each group of 4 sequences that share an index of batch, one has length 1024; one sequence of the whole batch has length 512. 2 <= split_point <= valid_length - 2 for each sequence.
All inputs are finite; a program needn't handle non-finite values.
Results may differ from a plain program's by a relative error of at most 0.033.
Values may be sent and summed in bfloat16 or wider, within the bound.
No kernel may reach another device: no remote copies, remote signals or barrier semaphores. Data moves between devices by JAX's collectives and lax.ppermute only.
A program may use at most 192 MiB of HBM per device.

v0:
```python
import math

import jax
import jax.numpy as jnp
from jax import lax
from jax.sharding import PartitionSpec as P

D = 384
HEADS = 12
HEAD_DIM = 32
TEACHER_HEAD_DIM = 64


NEG_LARGE = -1e30
NORM_EPS = 1e-12


def layer_norm(rows, gain, shift):
    center = jnp.mean(rows, axis=-1, keepdims=True)
    offsets = rows - center
    spread = jnp.mean(offsets * offsets, axis=-1, keepdims=True)
    return offsets * lax.rsqrt(spread + NORM_EPS) * gain + shift


def exact_gelu(values):
    return jax.nn.gelu(values, approximate=False)


def split_heads(rows, size):
    return rows.reshape(rows.shape[0], rows.shape[1] // size, size)


def row_spans(length):
    extent = min(512, length)
    return [(offset, extent) for offset in range(0, length, extent)]


def masked_scores(left, right, key_valid, factor):
    logits = jnp.einsum("qhd,khd->hqk", left, right, preferred_element_type=jnp.float32) * factor
    return jnp.where(key_valid[None, None, :], logits, NEG_LARGE)


def log_softmax(logits):
    highest = jnp.max(logits, axis=-1, keepdims=True)
    shifted = logits - highest
    return shifted - jnp.log(jnp.sum(jnp.exp(shifted), axis=-1, keepdims=True))


def project(rows, weight, biases):
    width = weight.shape[2]
    flat = jnp.einsum(
        "slw,wc->slc",
        rows,
        weight.reshape(weight.shape[0], 3 * width),
        preferred_element_type=jnp.float32,
    )
    queries = (flat[..., :width] + biases[0].astype(jnp.float32)).astype(jnp.bfloat16)
    key_rows = flat[..., width : 2 * width].astype(jnp.bfloat16)
    value_rows = (flat[..., 2 * width :] + biases[1].astype(jnp.float32)).astype(jnp.bfloat16)
    return (queries, key_rows, value_rows)


def bias_pair(gradients, width):
    column = jnp.sum(gradients, axis=(0, 1), dtype=jnp.float32)
    return jnp.stack((column[:width], column[2 * width :]))


def attend_forward(queries, key_rows, value_rows, key_valid, size):
    factor = 1.0 / math.sqrt(size)
    query_heads = split_heads(queries, size)
    key_heads = split_heads(key_rows, size)
    value_heads = split_heads(value_rows, size)
    outputs = []
    log_sums = []
    for offset, extent in row_spans(queries.shape[0]):
        logits = masked_scores(query_heads[offset : offset + extent], key_heads, key_valid, factor)
        highest = jnp.max(logits, axis=-1, keepdims=True)
        weights = jnp.exp(logits - highest)
        totals = jnp.sum(weights, axis=-1, keepdims=True)
        probability = (weights / totals).astype(jnp.bfloat16)
        mixing = jnp.einsum(
            "hqk,khd->qhd", probability, value_heads, preferred_element_type=jnp.float32
        )
        outputs.append(mixing.reshape(extent, -1).astype(jnp.bfloat16))
        log_sums.append((highest + jnp.log(totals))[..., 0])
    return (jnp.concatenate(outputs, axis=0), jnp.concatenate(log_sums, axis=1))


def attend_backward(queries, key_rows, value_rows, log_sums, grad_rows, key_valid, size):
    factor = 1.0 / math.sqrt(size)
    seq_rows = queries.shape[0]
    query_heads = split_heads(queries, size)
    key_heads = split_heads(key_rows, size)
    value_heads = split_heads(value_rows, size)
    grad_heads = split_heads(grad_rows, size)
    grad_keys = jnp.zeros(key_heads.shape, jnp.float32)
    grad_values = jnp.zeros(value_heads.shape, jnp.float32)
    grad_queries = []
    for offset, extent in row_spans(seq_rows):
        query_part = query_heads[offset : offset + extent]
        grad_part = grad_heads[offset : offset + extent]
        logits = masked_scores(query_part, key_heads, key_valid, factor)
        probability = jnp.exp(logits - log_sums[:, offset : offset + extent, None])
        grad_values = grad_values + jnp.einsum(
            "hqk,qhd->khd",
            probability.astype(jnp.bfloat16),
            grad_part,
            preferred_element_type=jnp.float32,
        )
        grad_prob = jnp.einsum(
            "qhd,khd->hqk", grad_part, value_heads, preferred_element_type=jnp.float32
        )
        grad_logits = (
            probability * (grad_prob - jnp.sum(grad_prob * probability, axis=-1, keepdims=True))
        ).astype(jnp.bfloat16)
        grad_queries.append(
            (
                jnp.einsum(
                    "hqk,khd->qhd", grad_logits, key_heads, preferred_element_type=jnp.float32
                )
                * factor
            ).reshape(extent, -1)
        )
        grad_keys = (
            grad_keys
            + jnp.einsum(
                "hqk,qhd->khd", grad_logits, query_part, preferred_element_type=jnp.float32
            )
            * factor
        )
    return (
        jnp.concatenate(grad_queries, axis=0),
        grad_keys.reshape(seq_rows, -1),
        grad_values.reshape(seq_rows, -1),
    )


def relation_grad(left, right, teacher_left, teacher_right, key_valid, row_weight):
    factor = 1.0 / math.sqrt(HEAD_DIM)
    teacher_factor = 1.0 / math.sqrt(TEACHER_HEAD_DIM)
    seq_rows = left.shape[0]
    left_heads = split_heads(left, HEAD_DIM)
    right_heads = split_heads(right, HEAD_DIM)
    teacher_lhs = split_heads(teacher_left, TEACHER_HEAD_DIM)
    teacher_rhs = split_heads(teacher_right, TEACHER_HEAD_DIM)
    divergence = jnp.zeros((), jnp.float32)
    grad_right = jnp.zeros(right_heads.shape, jnp.float32)
    grad_left = []
    for offset, extent in row_spans(seq_rows):
        left_part = left_heads[offset : offset + extent]
        student_log = log_softmax(masked_scores(left_part, right_heads, key_valid, factor))
        teacher_log = log_softmax(
            masked_scores(
                teacher_lhs[offset : offset + extent], teacher_rhs, key_valid, teacher_factor
            )
        )
        teacher_prob = jnp.exp(teacher_log)
        diverge = jnp.sum(
            jnp.where(key_valid[None, None, :], teacher_prob * (teacher_log - student_log), 0.0),
            axis=-1,
        )
        weight_part = row_weight[offset : offset + extent]
        divergence = divergence + jnp.sum(diverge * weight_part[None, :])
        grad_logits = ((jnp.exp(student_log) - teacher_prob) * weight_part[None, :, None]).astype(
            jnp.bfloat16
        )
        grad_left.append(
            (
                jnp.einsum(
                    "hqk,khd->qhd", grad_logits, right_heads, preferred_element_type=jnp.float32
                )
                * factor
            ).reshape(extent, -1)
        )
        grad_right = (
            grad_right
            + jnp.einsum("hqk,qhd->khd", grad_logits, left_part, preferred_element_type=jnp.float32)
            * factor
        )
    return (divergence, jnp.concatenate(grad_left, axis=0), grad_right.reshape(seq_rows, -1))


def body(
    student_rows,
    teacher_rows,
    valid_length,
    split_point,
    project_five,
    bias_five,
    output_five,
    branch_bias,
    norm_gain,
    norm_bias,
    widen_weight,
    widen_bias,
    narrow_weight,
    project_six,
    bias_six,
    teacher_project,
    teacher_bias,
):
    own_count = student_rows.shape[0]
    first_seq = lax.axis_index("heads") * own_count
    all_seqs = own_count * lax.axis_size("heads") * lax.axis_size("batch")
    own_lengths = lax.dynamic_slice_in_dim(valid_length, first_seq, own_count)
    weights = (
        project_five,
        bias_five,
        output_five,
        widen_weight,
        widen_bias,
        narrow_weight,
        project_six,
        bias_six,
        teacher_project,
        teacher_bias,
    )
    (
        wqkv_five,
        bqv_five,
        fifth_output_weight,
        widening_weight,
        b_widen,
        narrowing_weight,
        wqkv_six,
        bqv_six,
        wqkv_teacher,
        bqv_teacher,
    ) = weights
    incoming_rows = lax.all_gather(student_rows, "heads", axis=0, tiled=True)
    rows_teacher = lax.all_gather(teacher_rows, "heads", axis=0, tiled=True)
    seq_len = incoming_rows.shape[1]
    positions = jnp.arange(seq_len, dtype=jnp.int32)[None, :]
    key_valid = positions < valid_length[:, None]
    loss_rows = (
        key_valid
        & (positions != 0)
        & (positions != split_point[:, None] - 1)
        & (positions != valid_length[:, None] - 1)
    )
    row_weight = jnp.where(loss_rows, 1.0, 0.0).astype(jnp.float32) / (
        (valid_length - 3).astype(jnp.float32)[:, None] * float(all_seqs * HEADS)
    )
    queries, key_rows, value_rows = project(incoming_rows, wqkv_five, bqv_five)

    def forward_one(inputs):
        return attend_forward(inputs[0], inputs[1], inputs[2], inputs[3], HEAD_DIM)

    attended_rows, log_sums = lax.map(forward_one, (queries, key_rows, value_rows, key_valid))
    mixing = (
        lax.psum_scatter(
            jnp.einsum(
                "uor,re->uoe",
                attended_rows,
                fifth_output_weight,
                preferred_element_type=jnp.float32,
            ),
            "heads",
            scatter_dimension=0,
            tiled=True,
        )
        + branch_bias[0]
    )
    own_in = student_rows.astype(jnp.float32)
    middle, norm_one = jax.vjp(layer_norm, own_in + mixing, norm_gain[0], norm_bias[0])
    middle_low = middle.astype(jnp.bfloat16)
    middle_rows_values = lax.all_gather(middle_low, "heads", axis=0, tiled=True)
    pre_act = jnp.einsum(
        "bnz,zu->bnu", middle_rows_values, widening_weight, preferred_element_type=jnp.float32
    ) + b_widen.astype(jnp.float32)
    activated, gelu_back = jax.vjp(exact_gelu, pre_act)
    activation_reduced = activated.astype(jnp.bfloat16)
    branch_two = (
        lax.psum_scatter(
            jnp.einsum(
                "aym,mj->ayj",
                activation_reduced,
                narrowing_weight,
                preferred_element_type=jnp.float32,
            ).astype(jnp.bfloat16),
            "heads",
            scatter_dimension=0,
            tiled=True,
        ).astype(jnp.float32)
        + branch_bias[1]
    )
    block, norm_two = jax.vjp(layer_norm, middle + branch_two, norm_gain[1], norm_bias[1])
    block_low = block.astype(jnp.bfloat16)
    block_row_values = lax.all_gather(block_low, "heads", axis=0, tiled=True)
    query_six, key_six, value_six = project(block_row_values, wqkv_six, bqv_six)
    teacher_query, teacher_key, teacher_value = project(rows_teacher, wqkv_teacher, bqv_teacher)

    def relate(inputs):
        loss_att, grad_query, grad_key = relation_grad(
            inputs[0], inputs[1], inputs[3], inputs[4], inputs[6], inputs[7]
        )
        loss_val, grad_one, grad_two = relation_grad(
            inputs[2], inputs[2], inputs[5], inputs[5], inputs[6], inputs[7]
        )
        return (loss_att + loss_val, grad_query, grad_key, grad_one + grad_two)

    divergence, grad_q_six, grad_k_six, grad_v_six = lax.map(
        relate,
        (
            query_six,
            key_six,
            value_six,
            teacher_query,
            teacher_key,
            teacher_value,
            key_valid,
            row_weight,
        ),
    )
    sixth_gradient = jnp.concatenate((grad_q_six, grad_k_six, grad_v_six), axis=-1).astype(
        jnp.bfloat16
    )
    width_six = wqkv_six.shape[2]
    sixth_flattened = wqkv_six.reshape(wqkv_six.shape[0], 3 * width_six)
    grad_wqkv_six = jnp.einsum(
        "heo,hea->oa", block_row_values, sixth_gradient, preferred_element_type=jnp.float32
    ).reshape(-1, 3, width_six)
    grad_bqv_six = bias_pair(sixth_gradient, width_six)
    d_block = lax.psum_scatter(
        jnp.einsum(
            "fkx,gx->fkg", sixth_gradient, sixth_flattened, preferred_element_type=jnp.float32
        ).astype(jnp.bfloat16),
        "heads",
        scatter_dimension=0,
        tiled=True,
    ).astype(jnp.float32)
    d_sum_two, grad_gain_two, grad_shift_two = norm_two(d_block)
    d_branch = d_sum_two.astype(jnp.bfloat16)
    branch_gradient_rows = lax.all_gather(d_branch, "heads", axis=0, tiled=True)
    grad_w_narrow = jnp.einsum(
        "nhx,nhk->xk", activation_reduced, branch_gradient_rows, preferred_element_type=jnp.float32
    )
    activation_gradient = jnp.einsum(
        "pzq,wq->pzw", branch_gradient_rows, narrowing_weight, preferred_element_type=jnp.float32
    )
    preactivation_gradient = gelu_back(activation_gradient)[0].astype(jnp.bfloat16)
    grad_b_widen = jnp.sum(preactivation_gradient, axis=(0, 1), dtype=jnp.float32)
    widen_weight_gradient = jnp.einsum(
        "uyo,uyg->og",
        middle_rows_values,
        preactivation_gradient,
        preferred_element_type=jnp.float32,
    )
    d_middle = d_sum_two + lax.psum_scatter(
        jnp.einsum(
            "mrz,wz->mrw",
            preactivation_gradient,
            widening_weight,
            preferred_element_type=jnp.float32,
        ).astype(jnp.bfloat16),
        "heads",
        scatter_dimension=0,
        tiled=True,
    ).astype(jnp.float32)
    d_sum_one, grad_gain_one, grad_shift_one = norm_one(d_middle)
    d_mixing = d_sum_one.astype(jnp.bfloat16)
    mixing_gradient_rows = lax.all_gather(d_mixing, "heads", axis=0, tiled=True)
    grad_wout = jnp.einsum(
        "xuk,xuo->ko", attended_rows, mixing_gradient_rows, preferred_element_type=jnp.float32
    )
    d_attended = jnp.einsum(
        "mky,fy->mkf", mixing_gradient_rows, fifth_output_weight, preferred_element_type=jnp.float32
    ).astype(jnp.bfloat16)

    def backward_one(inputs):
        return attend_backward(
            inputs[0], inputs[1], inputs[2], inputs[3], inputs[4], inputs[5], HEAD_DIM
        )

    grad_q_five, grad_k_five, grad_v_five = lax.map(
        backward_one, (queries, key_rows, value_rows, log_sums, d_attended, key_valid)
    )
    fifth_gradient = jnp.concatenate((grad_q_five, grad_k_five, grad_v_five), axis=-1).astype(
        jnp.bfloat16
    )
    width_five = wqkv_five.shape[2]
    fifth_flattened = wqkv_five.reshape(wqkv_five.shape[0], 3 * width_five)
    grad_wqkv_five = jnp.einsum(
        "heo,hea->oa", incoming_rows, fifth_gradient, preferred_element_type=jnp.float32
    ).reshape(-1, 3, width_five)
    grad_bqv_five = bias_pair(fifth_gradient, width_five)
    grad_in = d_sum_one + lax.psum_scatter(
        jnp.einsum(
            "fkx,gx->fkg", fifth_gradient, fifth_flattened, preferred_element_type=jnp.float32
        ).astype(jnp.bfloat16),
        "heads",
        scatter_dimension=0,
        tiled=True,
    ).astype(jnp.float32)
    own_valid = (positions < own_lengths[:, None]).astype(jnp.float32)[..., None]
    partials = jnp.stack(
        (
            jnp.sum(divergence),
            jnp.sum(own_valid * own_in * own_in),
            jnp.sum(own_valid * mixing * mixing),
            jnp.sum(own_valid * branch_two * branch_two),
            jnp.sum(own_valid),
        )
    )
    branch_grads = jnp.stack(
        (
            jnp.sum(d_mixing, axis=(0, 1), dtype=jnp.float32),
            jnp.sum(d_branch, axis=(0, 1), dtype=jnp.float32),
        )
    )
    shared = lax.psum(
        (
            partials,
            branch_grads,
            jnp.stack((grad_gain_one, grad_gain_two)),
            jnp.stack((grad_shift_one, grad_shift_two)),
        ),
        ("heads", "batch"),
    )
    pieces = (
        grad_wqkv_five,
        grad_bqv_five,
        grad_wout,
        widen_weight_gradient,
        grad_b_widen,
        grad_w_narrow,
        grad_wqkv_six,
        grad_bqv_six,
    )
    summed = lax.psum(
        (pieces[0], pieces[1], pieces[2], pieces[3], pieces[4], pieces[5], pieces[6], pieces[7]),
        "batch",
    )
    totals = shared[0]
    counted = totals[4] * D
    summary = jnp.stack(
        (
            totals[0],
            jnp.sqrt(totals[1] / counted),
            jnp.sqrt(totals[2] / counted),
            jnp.sqrt(totals[3] / counted),
        )
    )
    return (
        block_low,
        grad_in,
        summed[0],
        summed[1],
        summed[2],
        shared[1],
        shared[2],
        shared[3],
        summed[3],
        summed[4],
        summed[5],
        summed[6],
        summed[7],
        summary,
    )


def solution(mesh):
    return jax.shard_map(
        body,
        mesh=mesh,
        in_specs=(
            P(("batch", "heads"), None, None),
            P(("batch", "heads"), None, None),
            P("batch"),
            P("batch"),
            P(None, None, "heads"),
            P(None, "heads"),
            P("heads", None),
            P(),
            P(),
            P(),
            P(None, "heads"),
            P("heads"),
            P("heads", None),
            P(None, None, "heads"),
            P(None, "heads"),
            P(None, None, "heads"),
            P(None, "heads"),
        ),
        out_specs=(
            P(("batch", "heads"), None, None),
            P(("batch", "heads"), None, None),
            P(None, None, "heads"),
            P(None, "heads"),
            P("heads", None),
            P(),
            P(),
            P(),
            P(None, "heads"),
            P("heads"),
            P("heads", None),
            P(None, None, "heads"),
            P(None, "heads"),
            P(),
        ),
        check_vma=False,
    )
```

profile of v0, /device:TPU:0, one launch (start us, length us, event | category | flops | bytes accessed | tf_op | source)
XLA Modules:
  0.0 1688.2 jit_solution(18176021901816418429)
XLA Ops:
  9.5 66.4 %all-gather.7.cloned.1.call-done = bf16[4,1024,384]{2,1,0:T(8,128)(2,1)} async-done(((bf16[1,1024,384]{2,1,0:T(8,128)(2,1)}), bf16[4,1024,384]{2,1,0:T(8,128)(2,1)}) %all-gather.7.cloned.1.call-update) | async-done | bytes 3145744 | tf_op jit(solution)/shard_map/all_gather | solution.py:230
  79.8 45.7 %while.42 = (s32[]{:T(128)}, bf16[4,1024,96]{1,2,0:T(8,128)(2,1)}, f32[4,3,1024]{2,1,0:T(4,128)}, bf16[4,1024,96]{1,2,0:T(8,128)(2,1)S(1)}, pred[4,1024]{1,0:T(4...) while((s32[]{:T(128)}, bf16[4,1024,96]{1,2,0:T(8,128)(2,1)}, ...), condition=%wide.region_5.6_spmd, body=%wide.region_0.5_spmd.sunk | while | flops 440893440 | bytes 41423004 | solution.py:249
  125.5 5.5 fusion.176
  131.3 109.4 %reduce-scatter.6.cloned.1.call-done = f32[1,1024,384]{2,1,0:T(8,128)} async-done(((f32[4,1024,384]{2,1,0:T(8,128)}), f32[1,1024,384]{2,1,0:T(8,128)}) %reduce-scatter.6.cloned.1.call-update) | async-done | bytes 1572880 | tf_op jit(solution)/shard_map/reduce_scatter | solution.py:251
  244.5 63.9 %all-gather.9.cloned.1.call-done = bf16[4,1024,384]{2,1,0:T(8,128)(2,1)} async-done(((bf16[1,1024,384]{2,1,0:T(8,128)(2,1)}), bf16[4,1024,384]{2,1,0:T(8,128)(2,1)}) %all-gather.9.cloned.1.call-update) | async-done | bytes 3145744 | tf_op jit(solution)/shard_map/all_gather | solution.py:267
  308.4 5.8 fusion.168
  314.3 15.3 multiply_convert_fusion.6
  337.0 57.1 %reduce-scatter.8.cloned.1.call-done = bf16[1,1024,384]{2,1,0:T(8,128)(2,1)} async-done(((bf16[4,1024,384]{2,1,0:T(8,128)(2,1)}), bf16[1,1024,384]{2,1,0:T(8,128)(2,1)}) %reduce-scatter.8.cloned.1.call-update) | async-done | bytes 786448 | tf_op jit(solution)/shard_map/reduce_scatter | solution.py:274
  401.4 109.5 %all-gather.11.cloned.1.call-done = bf16[4,1024,768]{2,1,0:T(8,128)(2,1)} async-done(((bf16[1,1024,768]{2,1,0:T(8,128)(2,1)}), bf16[4,1024,768]{2,1,0:T(8,128)(2,1)}) %all-gather.11.cloned.1.call-update) | async-done | bytes 6291472 | tf_op jit(solution)/shard_map/all_gather | solution.py:231
  511.0 6.0 fusion.203
  521.1 53.6 %all-gather.13.cloned.1.call-done = bf16[4,1024,384]{2,1,0:T(8,128)(2,1)} async-done(((bf16[1,1024,384]{2,1,0:T(8,128)(2,1)}), bf16[4,1024,384]{2,1,0:T(8,128)(2,1)}) %all-gather.13.cloned.1.call-update) | async-done | bytes 3145744 | tf_op jit(solution)/shard_map/all_gather | solution.py:289
  583.8 580.8 %while.43 = (s32[]{:T(128)}, f32[4]{0:T(128)}, bf16[4,1024,96]{1,2,0:T(8,128)(2,1)}, bf16[4,1024,96]{1,2,0:T(8,128)(2,1)}, bf16[4,1024,96]{1,2,0:T(8,128)(2,1)},...) while((s32[]{:T(128)}, f32[4]{0:T(128)}, ...), condition=%wide.region_37.38_spmd, body=%wide.region_12.37_spmd.sunk | while | flops 2109061120 | bytes 274567488 | solution.py:302
  590.1 8.4 log_subtract_fusion.15
  598.5 4.3 fusion.453
  602.7 8.4 log_subtract_fusion.21
  613.1 4.2 fusion.449
  617.3 8.7 log_subtract_fusion.17
  626.0 4.2 fusion.451
  630.2 8.7 log_subtract_fusion.19
  645.0 8.4 log_subtract_fusion.20
  663.5 8.4 log_subtract_fusion.16
  675.9 8.4 log_subtract_fusion.18
  685.0 27.6 %select_reduce_fusion.5 = (f32[3,512]{1,0:T(4,128)S(1)}, f32[3,512]{1,0:T(4,128)S(1)}, f32[3,512]{1,0:T(4,128)S(1)}, f32[3,512]{1,0:T(4,128)}, bf16[3,512,1024]{...) fusion(f32[3,512,1024]{2,1,0:T(8,128)} %log_subtract_fusion.15,, ...), kind=kOutput, calls=%fused_computation.57.clone.1 | output fusion | flops 45609472 | bytes 62944256 | tf_op jit(solution)/shard_map/while/body/eval_jaxpr/reduce_sum | solution.py:46
  733.5 8.4 log_subtract_fusion.15
  741.9 4.3 fusion.453
  746.1 8.4 log_subtract_fusion.21
  756.5 4.2 fusion.449
  760.7 8.7 log_subtract_fusion.17
  773.6 8.7 log_subtract_fusion.19
  788.3 8.4 log_subtract_fusion.20
  806.8 8.4 log_subtract_fusion.16
  819.2 8.4 log_subtract_fusion.18
  828.4 27.6 %select_reduce_fusion.5 = (f32[3,512]{1,0:T(4,128)S(1)}, f32[3,512]{1,0:T(4,128)S(1)}, f32[3,512]{1,0:T(4,128)S(1)}, f32[3,512]{1,0:T(4,128)}, bf16[3,512,1024]{...) fusion(f32[3,512,1024]{2,1,0:T(8,128)} %log_subtract_fusion.15,, ...), kind=kOutput, calls=%fused_computation.57.clone.1 | output fusion | flops 45609472 | bytes 62944256 | tf_op jit(solution)/shard_map/while/body/eval_jaxpr/reduce_sum | solution.py:46
  876.8 8.4 log_subtract_fusion.15
  885.2 4.3 fusion.453
  889.5 8.4 log_subtract_fusion.21
  899.8 4.2 fusion.449
  904.1 8.7 log_subtract_fusion.17
  916.9 8.7 log_subtract_fusion.19
  931.7 8.4 log_subtract_fusion.20
  950.2 8.4 log_subtract_fusion.16
  962.6 8.4 log_subtract_fusion.18
  971.8 27.6 %select_reduce_fusion.5 = (f32[3,512]{1,0:T(4,128)S(1)}, f32[3,512]{1,0:T(4,128)S(1)}, f32[3,512]{1,0:T(4,128)S(1)}, f32[3,512]{1,0:T(4,128)}, bf16[3,512,1024]{...) fusion(f32[3,512,1024]{2,1,0:T(8,128)} %log_subtract_fusion.15,, ...), kind=kOutput, calls=%fused_computation.57.clone.1 | output fusion | flops 45609472 | bytes 62944256 | tf_op jit(solution)/shard_map/while/body/eval_jaxpr/reduce_sum | solution.py:46
  1020.2 8.4 log_subtract_fusion.15
  1028.6 4.3 fusion.453
  1032.8 8.4 log_subtract_fusion.21
  1043.2 4.2 fusion.449
  1047.4 8.7 log_subtract_fusion.17
  1060.3 8.7 log_subtract_fusion.19
  1075.1 8.4 log_subtract_fusion.20
  1093.6 8.4 log_subtract_fusion.16
  1106.0 8.4 log_subtract_fusion.18
  1115.1 27.6 %select_reduce_fusion.5 = (f32[3,512]{1,0:T(4,128)S(1)}, f32[3,512]{1,0:T(4,128)S(1)}, f32[3,512]{1,0:T(4,128)S(1)}, f32[3,512]{1,0:T(4,128)}, bf16[3,512,1024]{...) fusion(f32[3,512,1024]{2,1,0:T(8,128)} %log_subtract_fusion.15,, ...), kind=kOutput, calls=%fused_computation.57.clone.1 | output fusion | flops 45609472 | bytes 62944256 | tf_op jit(solution)/shard_map/while/body/eval_jaxpr/reduce_sum | solution.py:46
  1164.6 5.6 convolution_convert_fusion.3
  1170.2 59.0 %reduce-scatter.10.cloned.1.call-done = bf16[1,1024,384]{2,1,0:T(8,128)(2,1)} async-done(((bf16[4,1024,384]{2,1,0:T(8,128)(2,1)}), bf16[1,1024,384]{2,1,0:T(8,128)(2,1)}) %reduce-scatter.10.cloned.1.call-update) | async-done | bytes 786448 | tf_op jit(solution)/shard_map/reduce_scatter | solution.py:324
  1235.2 63.6 %all-gather.15.cloned.1.call-done = bf16[4,1024,384]{2,1,0:T(8,128)(2,1)} async-done(((bf16[1,1024,384]{2,1,0:T(8,128)(2,1)}), bf16[4,1024,384]{2,1,0:T(8,128)(2,1)}) %all-gather.15.cloned.1.call-update) | async-done | bytes 3145744 | tf_op jit(solution)/shard_map/all_gather | solution.py:334
  1298.8 9.4 convert_reduce_fusion
  1313.8 59.0 %reduce-scatter.12.cloned.1.call-done = bf16[1,1024,384]{2,1,0:T(8,128)(2,1)} async-done(((bf16[4,1024,384]{2,1,0:T(8,128)(2,1)}), bf16[1,1024,384]{2,1,0:T(8,128)(2,1)}) %reduce-scatter.12.cloned.1.call-update) | async-done | bytes 786448 | tf_op jit(solution)/shard_map/reduce_scatter | solution.py:349
  1380.4 63.6 %all-gather.17.cloned.1.call-done = bf16[4,1024,384]{2,1,0:T(8,128)(2,1)} async-done(((bf16[1,1024,384]{2,1,0:T(8,128)(2,1)}), bf16[4,1024,384]{2,1,0:T(8,128)(2,1)}) %all-gather.17.cloned.1.call-update) | async-done | bytes 3145744 | tf_op jit(solution)/shard_map/all_gather | solution.py:362
  1450.1 87.6 %while.44 = (s32[]{:T(128)}, bf16[4,1024,96]{1,2,0:T(8,128)(2,1)}, bf16[4,1024,96]{1,2,0:T(8,128)(2,1)}, bf16[4,1024,96]{1,2,0:T(8,128)(2,1)}, bf16[4,1024,96]{1...) while((s32[]{:T(128)}, bf16[4,1024,96]{1,2,0:T(8,128)(2,1)}, ...), condition=%wide.region_47.48_spmd, body=%wide.region_44.47_spmd.sunk | while | flops 1054897152 | bytes 113954024 | solution.py:375
  1537.7 5.6 convolution_convert_fusion.2
  1564.9 43.1 %all-reduce = (f32[2,384]{1,0:T(2,128)}, f32[2,384]{1,0:T(2,128)}, f32[2,384]{1,0:T(2,128)}, f32[5]{0:T(128)S(1)}) all-reduce(f32[2,384]{1,0:T(2,128)S(1)} %pad_maximum_fusion.2, f32[2,384]{1,0:T(2,128)S(1)} %pad_maximum_fusion.3, f32[2,384]{1,0:T(2,128)S(1)} %pad_maximum_fusion.4, ...), channel_id=1, replica_groups=mesh['heads'=4,'batch'=8] {'heads','batch'}, use_global_device_ids=true, to_apply=%region_55.56 | all-reduce | flops 2309 | bytes 18472 | tf_op jit(solution)/shard_map/psum | solution.py:411
  1614.4 13.8 all-reduce.1
  1630.8 41.1 %all-reduce.5.cloned.1.call-done = (f32[384,3,96]{0,2,1:T(8,128)}, f32[96,384]{1,0:T(8,128)}, f32[384,384]{1,0:T(8,128)}, f32[384,384]{1,0:T(8,128)}, f32[384,3,96]{0,2,1:T(8,128)}) async-done(((f32[384,3,96]{0,2,1:T(8,128)}, f32[96,384]{1,0:T(8,128)}, f32[384,384]{1,0:T(8,128)}, f32[384,384]{1,0:T(8,128)}, f32[384,3,96]{0,2,1:T(8,128)}), (f32[384,3,96]{0,2,1:T(8,128)}, f32[96,384]{1,0:T(8,128)}, ...) | async-done | bytes 2211856 | tf_op jit(solution)/shard_map/psum | solution.py:430
  (608 shorter events, 408.8 us)
Async XLA Ops:
  7.2 503.8 %copy-start = (bf16[768,3,192]{0,2,1:T(8,128)(2,1)S(1)}, bf16[768,3,192]{0,2,1:T(8,128)(2,1)}, u32[]{:S(2)}) copy-start(bf16[768,3,192]{0,2,1:T(8,128)(2,1)} %param.38) | copy-start | bytes 2654212
  7.2 68.6 %all-gather.7.cloned.1.call-start = ((), (), s32[]{:S(2)}) async-start(), calls=%async_computation.5 | async-start | bytes 3932160 | tf_op jit(solution)/shard_map/all_gather | solution.py:230
  7.9 232.7 %reduce-scatter.6.cloned.1.call-start = ((), (), s32[]{:S(2)}) async-start(), calls=%async_computation.6 | async-start | bytes 7864320 | tf_op jit(solution)/shard_map/reduce_scatter | solution.py:251
  131.1 113.5 %copy-start.77 = (bf16[384]{0:T(512)(128)(2,1)S(1)}, bf16[384]{0:T(512)(128)(2,1)}, u32[]{:S(2)}) copy-start(bf16[384]{0:T(512)(128)(2,1)} %param.34) | copy-start | bytes 2308
  131.1 177.3 %all-gather.9.cloned.1.call-start = ((), (), s32[]{:S(2)}) async-start(), calls=%async_computation.7 | async-start | bytes 3932160 | tf_op jit(solution)/shard_map/all_gather | solution.py:267
  131.2 262.9 %copy-start.52 = (f32[384]{0:T(512)}, f32[384]{0:T(512)S(1)}, u32[]{:S(2)}) copy-start(f32[384]{0:T(512)S(1)} %get-tuple-element.362) | copy-start | bytes 4612
  131.3 267.6 %copy-start.60 = (f32[384]{0:T(512)}, f32[384]{0:T(512)S(1)}, u32[]{:S(2)}) copy-start(f32[384]{0:T(512)S(1)} %get-tuple-element.363) | copy-start | bytes 4612
  242.6 151.6 %copy-start.4 = (f32[1,1024,384]{2,1,0:T(8,128)}, f32[1,1024,384]{2,1,0:T(8,128)S(1)}, u32[]{:S(2)}) copy-start(f32[1,1024,384]{2,1,0:T(8,128)S(1)} %get-tuple-element.299) | copy-start | bytes 4718596
  242.6 151.6 %copy-start.44 = (f32[1024]{0:T(1024)}, f32[1024]{0:T(1024)S(1)}, u32[]{:S(2)}) copy-start(f32[1024]{0:T(1024)S(1)} %broadcast_multiply_fusion.1) | copy-start | bytes 12292
  243.0 71.3 %copy-start.56 = (f32[1024]{0:T(1024)}, f32[1024]{0:T(1024)S(1)}, u32[]{:S(2)}) copy-start(f32[1024]{0:T(1024)S(1)} %multiply_reduce_fusion.9) | copy-start | bytes 12292
  243.0 151.2 %copy-start.48 = (f32[1024]{0:T(1024)}, f32[1024]{0:T(1024)S(1)}, u32[]{:S(2)}) copy-start(f32[1024]{0:T(1024)S(1)} %fusion.182) | copy-start | bytes 12292
  244.2 149.9 %reduce-scatter.8.cloned.1.call-start = ((), (), s32[]{:S(2)}) async-start(), calls=%async_computation.8 | async-start | bytes 3932160 | tf_op jit(solution)/shard_map/reduce_scatter | solution.py:274
  244.5 69.7 %copy-start.64 = (f32[384]{0:T(512)}, f32[384]{0:T(512)S(1)}, u32[]{:S(2)}) copy-start(f32[384]{0:T(512)S(1)} %convert_element_type.226) | copy-start | bytes 4612
  314.2 15.4 copy-start.27
  314.2 17.0 %copy-start.39 = (bf16[384,384]{1,0:T(8,128)(2,1)S(1)}, bf16[384,384]{1,0:T(8,128)(2,1)}, u32[]{:S(2)}) copy-start(bf16[384,384]{1,0:T(8,128)(2,1)} %param.35) | copy-start | bytes 884740
  331.3 62.9 %copy-start.26 = (bf16[1,1024,384]{2,1,0:T(8,128)(2,1)S(1)}, bf16[1,1024,384]{2,1,0:T(8,128)(2,1)}, u32[]{:S(2)}) copy-start(bf16[1,1024,384]{2,1,0:T(8,128)(2,1)} %param.23) | copy-start | bytes 2359300
  335.1 65.6 %copy-start.76 = (bf16[2,96]{1,0:T(2,128)(2,1)S(1)}, bf16[2,96]{1,0:T(2,128)(2,1)}, u32[]{:S(2)}) copy-start(bf16[2,96]{1,0:T(2,128)(2,1)} %param.37) | copy-start | bytes 1156
  335.1 65.6 %copy-start.78 = (s32[4]{0:T(128)S(1)}, s32[4]{0:T(128)}, u32[]{:S(2)}) copy-start(s32[4]{0:T(128)} %param.26) | copy-start | bytes 52
  335.1 65.6 %copy-start.71 = (bf16[2,192]{1,0:T(2,128)(2,1)S(1)}, bf16[2,192]{1,0:T(2,128)(2,1)}, u32[]{:S(2)}) copy-start(bf16[2,192]{1,0:T(2,128)(2,1)} %param.39) | copy-start | bytes 2308
  335.1 175.9 %all-gather.11.cloned.1.call-start = ((), (), s32[]{:S(2)}) async-start(), calls=%async_computation.9 | async-start | bytes 7864320 | tf_op jit(solution)/shard_map/all_gather | solution.py:231
  335.7 239.0 %all-gather.13.cloned.1.call-start = ((), (), s32[]{:S(2)}) async-start(), calls=%async_computation.10 | async-start | bytes 3932160 | tf_op jit(solution)/shard_map/all_gather | solution.py:289
  397.7 119.3 %copy-start.46 = (f32[1024]{0:T(1024)}, f32[1024]{0:T(1024)S(1)}, u32[]{:S(2)}) copy-start(f32[1024]{0:T(1024)S(1)} %broadcast_multiply_fusion) | copy-start | bytes 12292
  398.8 118.1 %copy-start.50 = (f32[1024]{0:T(1024)}, f32[1024]{0:T(1024)S(1)}, u32[]{:S(2)}) copy-start(f32[1024]{0:T(1024)S(1)} %fusion.183) | copy-start | bytes 12292
  400.1 829.1 %reduce-scatter.10.cloned.1.call-start = ((), (), s32[]{:S(2)}) async-start(), calls=%async_computation.11 | async-start | bytes 3932160 | tf_op jit(solution)/shard_map/reduce_scatter | solution.py:324
  517.0 57.8 %copy-start.43 = (bf16[384,3,96]{0,2,1:T(8,128)(2,1)S(1)}, bf16[384,3,96]{0,2,1:T(8,128)(2,1)}, u32[]{:S(2)}) copy-start(bf16[384,3,96]{0,2,1:T(8,128)(2,1)} %param.36) | copy-start | bytes 663556
  584.9 13.6 copy-start.18
  584.9 13.5 copy-start.16
  612.1 14.0 copy-start.14
  612.1 13.9 copy-start.19
  728.3 13.6 copy-start.18
  728.3 13.5 copy-start.16
  755.4 14.0 copy-start.14
  755.4 13.9 copy-start.19
  871.7 13.6 copy-start.18
  871.7 13.5 copy-start.16
  898.8 13.9 copy-start.14
  898.8 13.9 copy-start.19
  1015.0 13.6 copy-start.18
  1015.0 13.5 copy-start.16
  1042.2 14.0 copy-start.14
  1042.2 13.9 copy-start.19
  1164.5 64.7 %copy-start.7 = (f32[1,1024,384]{2,1,0:T(8,128)S(1)}, f32[1,1024,384]{2,1,0:T(8,128)}, u32[]{:S(2)}) copy-start(f32[1,1024,384]{2,1,0:T(8,128)} %copy-done.6) | copy-start | bytes 4718596
  1164.5 64.7 %copy-start.47 = (f32[1024]{0:T(1024)S(1)}, f32[1024]{0:T(1024)}, u32[]{:S(2)}) copy-start(f32[1024]{0:T(1024)} %copy-done.46) | copy-start | bytes 12292
  1164.5 64.7 %copy-start.51 = (f32[1024]{0:T(1024)S(1)}, f32[1024]{0:T(1024)}, u32[]{:S(2)}) copy-start(f32[1024]{0:T(1024)} %copy-done.50) | copy-start | bytes 12292
  1164.5 64.7 %copy-start.61 = (f32[384]{0:T(512)S(1)}, f32[384]{0:T(512)}, u32[]{:S(2)}) copy-start(f32[384]{0:T(512)} %copy-done.60) | copy-start | bytes 4612
  1164.6 67.1 %copy-start.59 = (f32[1024]{0:T(1024)S(1)}, f32[1024]{0:T(1024)}, u32[]{:S(2)}) copy-start(f32[1024]{0:T(1024)} %copy-done.58) | copy-start | bytes 12292
  1170.1 128.7 %copy-start.40 = (bf16[384,384]{1,0:T(8,128)(2,1)S(1)}, bf16[384,384]{1,0:T(8,128)(2,1)}, u32[]{:S(2)}) copy-start(bf16[384,384]{1,0:T(8,128)(2,1)} %param.35) | copy-start | bytes 884740
  1170.1 128.7 %copy-start.65 = (f32[384]{0:T(512)S(1)}, f32[384]{0:T(512)}, u32[]{:S(2)}) copy-start(f32[384]{0:T(512)} %copy-done.64) | copy-start | bytes 4612
  1170.2 128.6 %all-gather.15.cloned.1.call-start = ((), (), s32[]{:S(2)}) async-start(), calls=%async_computation.12 | async-start | bytes 3932160 | tf_op jit(solution)/shard_map/all_gather | solution.py:334
  1235.1 137.7 %reduce-scatter.12.cloned.1.call-start = ((), (), s32[]{:S(2)}) async-start(), calls=%async_computation.13 | async-start | bytes 3932160 | tf_op jit(solution)/shard_map/reduce_scatter | solution.py:349
  1309.9 62.9 %copy-start.5 = (f32[1,1024,384]{2,1,0:T(8,128)S(1)}, f32[1,1024,384]{2,1,0:T(8,128)}, u32[]{:S(2)}) copy-start(f32[1,1024,384]{2,1,0:T(8,128)} %copy-done.4) | copy-start | bytes 4718596
  1309.9 62.9 %copy-start.45 = (f32[1024]{0:T(1024)S(1)}, f32[1024]{0:T(1024)}, u32[]{:S(2)}) copy-start(f32[1024]{0:T(1024)} %copy-done.44) | copy-start | bytes 12292
  1309.9 62.9 %copy-start.49 = (f32[1024]{0:T(1024)S(1)}, f32[1024]{0:T(1024)}, u32[]{:S(2)}) copy-start(f32[1024]{0:T(1024)} %copy-done.48) | copy-start | bytes 12292
  1309.9 62.9 %copy-start.53 = (f32[384]{0:T(512)S(1)}, f32[384]{0:T(512)}, u32[]{:S(2)}) copy-start(f32[384]{0:T(512)} %copy-done.52) | copy-start | bytes 4612
  1309.9 65.5 %copy-start.57 = (f32[1024]{0:T(1024)S(1)}, f32[1024]{0:T(1024)}, u32[]{:S(2)}) copy-start(f32[1024]{0:T(1024)} %copy-done.56) | copy-start | bytes 12292
  1313.8 130.3 %copy-start.42 = (bf16[96,384]{1,0:T(8,128)(2,1)S(1)}, bf16[96,384]{1,0:T(8,128)(2,1)}, u32[]{:S(2)}) copy-start(bf16[96,384]{1,0:T(8,128)(2,1)} %param.29) | copy-start | bytes 221188
  1313.8 130.3 %all-gather.17.cloned.1.call-start = ((), (), s32[]{:S(2)}) async-start(), calls=%async_computation.14 | async-start | bytes 3932160 | tf_op jit(solution)/shard_map/all_gather | solution.py:362
  1377.6 72.5 %copy-start.54 = (f32[1024]{0:T(1024)}, f32[1024]{0:T(1024)S(1)}, u32[]{:S(2)}) copy-start(f32[1024]{0:T(1024)S(1)} %negate_multiply_fusion.1) | copy-start | bytes 12292
  1380.4 247.8 %reduce-scatter.14.cloned.1.call-start = ((), (), s32[]{:S(2)}) async-start(), calls=%async_computation.15 | async-start | bytes 3932160 | tf_op jit(solution)/shard_map/reduce_scatter | solution.py:387
  1543.3 128.6 %all-reduce.5.cloned.1.call-start = ((), (), s32[]{:S(2)}) async-start(), calls=%async_computation.16 | async-start | bytes 4423680 | tf_op jit(solution)/shard_map/psum | solution.py:430
  1562.7 51.7 %copy-start.75 = (f32[384]{0:T(512)S(1)}, f32[384]{0:T(512)}, u32[]{:S(2)}) copy-start(f32[384]{0:T(512)} %get-tuple-element.360) | copy-start | bytes 4612
  1562.7 65.5 %copy-start.13 = (f32[1,1024,384]{2,1,0:T(8,128)S(1)}, f32[1,1024,384]{2,1,0:T(8,128)}, u32[]{:S(2)}) copy-start(f32[1,1024,384]{2,1,0:T(8,128)} %copy-done.12) | copy-start | bytes 4718596
  1562.7 65.5 %copy-start.55 = (f32[1024]{0:T(1024)S(1)}, f32[1024]{0:T(1024)}, u32[]{:S(2)}) copy-start(f32[1024]{0:T(1024)} %copy-done.54) | copy-start | bytes 12292
  1564.9 116.0 %copy-start.1 = (bf16[768,3,192]{0,2,1:T(8,128)(2,1)S(1)}, bf16[768,3,192]{0,2,1:T(8,128)(2,1)}, u32[]{:S(2)}) copy-start(bf16[768,3,192]{0,2,1:T(8,128)(2,1)} %param.38) | copy-start | bytes 2654212
  (78 other events, 316.1 us)
Sparse Core Ops, SparseCore 0:
  9.6 66.1 all-gather.6
  131.2 109.4 reduce-scatter.5
  244.4 64.0 all-gather.8
  335.2 58.8 reduce-scatter.7
  395.6 115.3 all-gather.10
  513.0 61.7 all-gather.12
  1170.3 58.8 reduce-scatter.9
  1235.2 63.5 all-gather.14
  1313.9 58.8 reduce-scatter.11
  1380.5 63.5 all-gather.16
  1543.4 59.8 reduce-scatter.13
  1608.2 63.6 all-reduce.4
where the time goes:
time: 1700 us; the launch traced here: 1690 us
  waiting for transfers between devices  748 us (44%)
  other arithmetic  435 us (26%)
  matrix products  322 us (19%)
  local copies, waits for them, and re-layouts  87.7 us (5%)
  blocking collectives  56.9 us (3%)
  loops' own time  19.2 us (1%)
  between operations  18.2 us (1%)
    reduce_sum x32, other arithmetic, log_softmax(): return shifted - jnp.log(jnp.sum(jnp.exp(shifted), axis=-1, keepdims=True))  347 us
    sub x32, matrix products, log_softmax(): shifted = logits - highest  131 us
    all_gather x1, waiting for transfers between devices, body(): rows_teacher = lax.all_gather(teacher_rows, 'heads', axis=0, tiled=True)  110 us
    reduce_scatter x1, waiting for transfers between devices, body(): lax.psum_scatter(jnp.einsum('uor,re->uoe', attended_rows, fifth_output_we...  109 us
    all_gather x1, waiting for transfers between devices, body(): incoming_rows = lax.all_gather(student_rows, 'heads', axis=0, tiled=True)  66.4 us
    all_gather x1, waiting for transfers between devices, body(): middle_rows_values = lax.all_gather(middle_low, 'heads', axis=0, tiled=True)  63.9 us
    all_gather x1, waiting for transfers between devices, body(): branch_gradient_rows = lax.all_gather(d_branch, 'heads', axis=0, tiled=True)  63.6 us
    all_gather x1, waiting for transfers between devices, body(): mixing_gradient_rows = lax.all_gather(d_mixing, 'heads', axis=0, tiled=True)  63.6 us
  transfers between devices with their start and end apart: 12, of which 11 were waited for; matrix products, arithmetic and copies ran while one was open for 3% of the time, Pallas kernels for 0%

commit v1 on v0

v1 whole, which is shorter than its diff:
```python
import functools
import math

import jax
import jax.numpy as jnp
from jax import lax
from jax.experimental import pallas as pl
from jax.experimental.pallas import tpu as pltpu
from jax.sharding import PartitionSpec as P

D = 384
HEADS = 12
HEAD_DIM = 32
TEACHER_HEAD_DIM = 64
GROUP = 4
TILE = 256
NORM_EPS = 1e-12
MASKED = -1e30
LOG2E = math.log2(math.e)
LN2 = math.log(2.0)
STUDENT_SCALE = 1.0 / math.sqrt(HEAD_DIM)
TEACHER_SCALE = 1.0 / math.sqrt(TEACHER_HEAD_DIM)
VMEM = 56 * 2**20

f32 = jnp.float32
bf16 = jnp.bfloat16

NN = (((1,), (0,)), ((), ()))
NT = (((1,), (1,)), ((), ()))


def dot(left, right, dims=NN):
    return lax.dot_general(left, right, dims, preferred_element_type=f32)


def lanes(shape):
    return lax.broadcasted_iota(jnp.int32, shape, 1)


def split_rows(rows, head, size, scale):
    lane = lanes(rows.shape)
    inside = (lane >= head * size) & (lane < (head + 1) * size)
    extra = lax.rem(head + 1, 128 // size) * size
    scaled = rows.astype(f32) * scale
    high = scaled.astype(bf16).astype(f32)
    low = scaled - high
    first = jnp.where(inside, high, jnp.where(lane == extra, 1.0, 0.0))
    second = jnp.where(inside, low, 0.0)
    return jnp.concatenate([first.astype(bf16), second.astype(bf16)], axis=1)


def key_columns(rows, head, size, bias):
    lane = lanes(rows.shape)
    extra = lax.rem(head + 1, 128 // size) * size
    wide = rows.astype(f32)
    return jnp.concatenate([jnp.where(lane == extra, bias, wide).astype(bf16), rows], axis=1)


def key_bias(rows, length):
    position = lax.broadcasted_iota(jnp.int32, (rows, 1), 0)
    return jnp.where(position < length, 0.0, MASKED)


def attend_forward_kernel(length_ref, q_ref, k_ref, v_ref, e_ref, r_ref, o_ref, lhs, rhs):
    rows = q_ref.shape[0]
    tile = min(TILE, rows)
    bias = key_bias(rows, length_ref[0])

    def one_head(head, carry):
        lhs[...] = split_rows(q_ref[...], head, HEAD_DIM, STUDENT_SCALE * LOG2E)
        rhs[...] = key_columns(k_ref[...], head, HEAD_DIM, bias)

        def one_tile(step, carry):
            span = pl.ds(pl.multiple_of(step * tile, tile), tile)
            logits = dot(lhs[span, :], rhs[...], NT)
            weights = jnp.exp2(logits - jnp.max(logits, axis=1, keepdims=True))
            inverse = 1.0 / jnp.sum(weights, axis=1, keepdims=True)
            low = weights.astype(bf16)
            e_ref[head, span, :] = low
            mixed = dot(low, v_ref[...]) * inverse
            lane = lanes(mixed.shape)
            inside = (lane >= head * HEAD_DIM) & (lane < (head + 1) * HEAD_DIM)
            o_ref[span, :] = jnp.where(inside, mixed, o_ref[span, :].astype(f32)).astype(bf16)
            r_ref[span, :] = jnp.where(inside, inverse, r_ref[span, :])
            return carry

        return lax.fori_loop(0, rows // tile, one_tile, carry)

    lax.fori_loop(0, GROUP, one_head, 0)


def attend_forward(length, q, k, v):
    rows, width = q.shape
    groups = width // 128
    wide = pl.BlockSpec((rows, 128), lambda g: (0, g))
    return pl.pallas_call(
        attend_forward_kernel,
        grid=(groups,),
        in_specs=[pl.BlockSpec(memory_space=pltpu.SMEM), wide, wide, wide],
        out_specs=[pl.BlockSpec((GROUP, rows, rows), lambda g: (g, 0, 0)), wide, wide],
        out_shape=[
            jax.ShapeDtypeStruct((groups * GROUP, rows, rows), bf16),
            jax.ShapeDtypeStruct((rows, width), f32),
            jax.ShapeDtypeStruct((rows, width), bf16),
        ],
        scratch_shapes=[pltpu.VMEM((rows, 256), bf16), pltpu.VMEM((rows, 256), bf16)],
        compiler_params=pltpu.CompilerParams(vmem_limit_bytes=VMEM),
        name="attend_forward",
    )(length, q, k, v)


def attend_backward_kernel(
    q_ref, k_ref, v_ref, e_ref, r_ref, a_ref, d_ref, dq_ref, dk_ref, dv_ref, lhs, rhs, qt, dt, dkt, dvt
):
    rows = q_ref.shape[0]
    tile = min(TILE, rows)
    scaled = r_ref[...] * d_ref[...].astype(f32)
    qt[...] = q_ref[...].T
    dt[...] = scaled.astype(bf16).T
    dkt[...] = jnp.zeros_like(dkt)
    dvt[...] = jnp.zeros_like(dvt)

    def one_head(head, carry):
        lane = lanes((rows, 128))
        inside = (lane >= head * HEAD_DIM) & (lane < (head + 1) * HEAD_DIM)
        extra = lax.rem(head + 1, GROUP) * HEAD_DIM
        grads = r_ref[...] * d_ref[...].astype(f32)
        shift = -jnp.sum(jnp.where(inside, grads * a_ref[...].astype(f32), 0.0), axis=1, keepdims=True)
        high = grads.astype(bf16).astype(f32)
        shift_high = shift.astype(bf16).astype(f32)
        spare = jnp.where(lane == extra, shift_high, jnp.where(lane == extra + 1, shift - shift_high, 0.0))
        lhs[...] = jnp.concatenate(
            [
                jnp.where(inside, high, spare).astype(bf16),
                jnp.where(inside, grads - high, 0.0).astype(bf16),
            ],
            axis=1,
        )
        ones = (lane == extra) | (lane == extra + 1)
        rhs[...] = jnp.concatenate(
            [jnp.where(ones, 1.0, v_ref[...].astype(f32)).astype(bf16), v_ref[...]], axis=1
        )
        head_rows = pl.ds(pl.multiple_of(head * HEAD_DIM, HEAD_DIM), HEAD_DIM)

        def one_tile(step, carry):
            span = pl.ds(pl.multiple_of(step * tile, tile), tile)
            weights = e_ref[head, span, :]
            change = dot(lhs[span, :], rhs[...], NT)
            grad = (weights.astype(f32) * change).astype(bf16)
            found = dot(grad, k_ref[...]) * STUDENT_SCALE
            here = lanes(found.shape)
            held = (here >= head * HEAD_DIM) & (here < (head + 1) * HEAD_DIM)
            dq_ref[span, :] = jnp.where(held, found, dq_ref[span, :].astype(f32)).astype(bf16)
            dkt[head_rows, :] += dot(qt[head_rows, span], grad)
            dvt[head_rows, :] += dot(dt[head_rows, span], weights)
            return carry

        return lax.fori_loop(0, rows // tile, one_tile, carry)

    lax.fori_loop(0, GROUP, one_head, 0)
    dk_ref[...] = (dkt[...] * STUDENT_SCALE).T.astype(bf16)
    dv_ref[...] = dvt[...].T.astype(bf16)


def attend_backward(q, k, v, e, r, attended, d_attended):
    rows, width = q.shape
    groups = width // 128
    wide = pl.BlockSpec((rows, 128), lambda g: (0, g))
    return pl.pallas_call(
        attend_backward_kernel,
        grid=(groups,),
        in_specs=[wide, wide, wide, pl.BlockSpec((GROUP, rows, rows), lambda g: (g, 0, 0)), wide, wide, wide],
        out_specs=[wide, wide, wide],
        out_shape=[jax.ShapeDtypeStruct((rows, width), bf16)] * 3,
        scratch_shapes=[
            pltpu.VMEM((rows, 256), bf16),
            pltpu.VMEM((rows, 256), bf16),
            pltpu.VMEM((128, rows), bf16),
            pltpu.VMEM((128, rows), bf16),
            pltpu.VMEM((128, rows), f32),
            pltpu.VMEM((128, rows), f32),
        ],
        compiler_params=pltpu.CompilerParams(vmem_limit_bytes=VMEM),
        name="attend_backward",
    )(q, k, v, e, r, attended, d_attended)


def relation_kernel(
    length_ref, q_ref, k_ref, v_ref, tq_ref, tk_ref, tv_ref, w_ref,
    dq_ref, dk_ref, dv_ref, kl_ref, lhs, rhs, tlhs, trhs, lt, right_t, left_sum,
):
    rows = q_ref.shape[0]
    tile = min(TILE, rows)
    bias = key_bias(rows, length_ref[0])

    @pl.when(pl.program_id(0) == 0)
    def _():
        kl_ref[...] = jnp.zeros_like(kl_ref)

    def relate(left_ref, right_ref, tleft_ref, tright_ref):
        lt[...] = left_ref[...].T
        right_t[...] = jnp.zeros_like(right_t)

        def one_head(head, carry):
            lhs[...] = split_rows(left_ref[...], head, HEAD_DIM, STUDENT_SCALE * LOG2E)
            rhs[...] = key_columns(right_ref[...], head, HEAD_DIM, bias)
            part = pl.ds(pl.multiple_of((head // 2) * 128, 128), 128)
            own = lax.rem(head, 2)
            tlhs[...] = split_rows(tleft_ref[:, part], own, TEACHER_HEAD_DIM, TEACHER_SCALE * LOG2E)
            trhs[...] = key_columns(tright_ref[:, part], own, TEACHER_HEAD_DIM, bias)
            head_rows = pl.ds(pl.multiple_of(head * HEAD_DIM, HEAD_DIM), HEAD_DIM)

            def one_tile(step, carry):
                span = pl.ds(pl.multiple_of(step * tile, tile), tile)
                student = dot(lhs[span, :], rhs[...], NT)
                student = student - jnp.max(student, axis=1, keepdims=True)
                teacher = dot(tlhs[span, :], trhs[...], NT)
                teacher = teacher - jnp.max(teacher, axis=1, keepdims=True)
                es = jnp.exp2(student)
                et = jnp.exp2(teacher)
                sum_s = jnp.sum(es, axis=1, keepdims=True)
                sum_t = jnp.sum(et, axis=1, keepdims=True)
                cross = jnp.sum(et * (teacher - student), axis=1, keepdims=True)
                weight = w_ref[span, :]
                kl_ref[span, :] += weight * (LN2 * cross / sum_t + jnp.log(sum_s) - jnp.log(sum_t))
                grad = (es * (weight / sum_s) - et * (weight / sum_t)).astype(bf16)
                found = dot(grad, right_ref[...]) * STUDENT_SCALE
                here = lanes(found.shape)
                held = (here >= head * HEAD_DIM) & (here < (head + 1) * HEAD_DIM)
                left_sum[span, :] = jnp.where(held, found, left_sum[span, :])
                right_t[head_rows, :] += dot(lt[head_rows, span], grad)
                return carry

            return lax.fori_loop(0, rows // tile, one_tile, carry)

        lax.fori_loop(0, GROUP, one_head, 0)

    relate(q_ref, k_ref, tq_ref, tk_ref)
    dq_ref[...] = left_sum[...].astype(bf16)
    dk_ref[...] = (right_t[...] * STUDENT_SCALE).T.astype(bf16)
    relate(v_ref, v_ref, tv_ref, tv_ref)
    dv_ref[...] = (left_sum[...] + (right_t[...] * STUDENT_SCALE).T).astype(bf16)


def relations(length, q, k, v, tq, tk, tv, weight):
    rows, width = q.shape
    groups = width // 128
    wide = pl.BlockSpec((rows, 128), lambda g: (0, g))
    double = pl.BlockSpec((rows, 256), lambda g: (0, g))
    single = pl.BlockSpec((rows, 1), lambda g: (0, 0))
    return pl.pallas_call(
        relation_kernel,
        grid=(groups,),
        in_specs=[pl.BlockSpec(memory_space=pltpu.SMEM), wide, wide, wide, double, double, double, single],
        out_specs=[wide, wide, wide, single],
        out_shape=[jax.ShapeDtypeStruct((rows, width), bf16)] * 3 + [jax.ShapeDtypeStruct((rows, 1), f32)],
        scratch_shapes=[
            pltpu.VMEM((rows, 256), bf16),
            pltpu.VMEM((rows, 256), bf16),
            pltpu.VMEM((rows, 256), bf16),
            pltpu.VMEM((rows, 256), bf16),
            pltpu.VMEM((128, rows), bf16),
            pltpu.VMEM((128, rows), f32),
            pltpu.VMEM((rows, 128), f32),
        ],
        compiler_params=pltpu.CompilerParams(vmem_limit_bytes=VMEM),
        name="relations",
    )(length, q, k, v, tq, tk, tv, weight)


def project(rows, weight, biases):
    width = weight.shape[2]
    flat = dot(rows, weight.reshape(weight.shape[0], 3 * width))
    q = (flat[:, :width] + biases[0].astype(f32)).astype(bf16)
    k = flat[:, width : 2 * width].astype(bf16)
    v = (flat[:, 2 * width :] + biases[1].astype(f32)).astype(bf16)
    return q, k, v


def norm_forward(rows, gain, shift):
    center = jnp.mean(rows, axis=-1, keepdims=True)
    offsets = rows - center
    rstd = lax.rsqrt(jnp.mean(offsets * offsets, axis=-1, keepdims=True) + NORM_EPS)
    normed = offsets * rstd
    return normed * gain + shift, normed, rstd


def norm_backward(grad, normed, rstd, gain):
    inner = grad * gain
    mean = jnp.mean(inner, axis=-1, keepdims=True)
    slope = jnp.mean(inner * normed, axis=-1, keepdims=True)
    down = rstd * (inner - mean - normed * slope)
    return down, jnp.sum(grad * normed, axis=0), jnp.sum(grad, axis=0)


def exact_gelu(values):
    return jax.nn.gelu(values, approximate=False)


def reduce_pieces(pieces):
    shares = pieces[0].shape[0]
    batch = lax.axis_size("batch")
    flat = jnp.concatenate([p.astype(bf16).reshape(shares, -1) for p in pieces], axis=1)
    size = flat.shape[1]
    pad = -size % (batch * 128)
    if pad:
        flat = jnp.pad(flat, ((0, 0), (0, pad)))
    flat = lax.psum_scatter(flat, "batch", scatter_dimension=1, tiled=True)
    flat = lax.psum_scatter(flat, "heads", scatter_dimension=0, tiled=True)
    flat = lax.all_gather(flat, "batch", axis=1, tiled=True)[0].astype(f32)
    out = []
    offset = 0
    for p in pieces:
        count = math.prod(p.shape[1:])
        out.append(flat[offset : offset + count].reshape(p.shape[1:]))
        offset += count
    return out


def body(
    student_rows, teacher_rows, valid_length, split_point, project_five, bias_five, output_five, branch_bias,
    norm_gain, norm_bias, widen_weight, widen_bias, narrow_weight, project_six, bias_six, teacher_project,
    teacher_bias,
):
    shares = lax.axis_size("heads")
    me = lax.axis_index("heads")
    all_seqs = shares * lax.axis_size("batch")
    x = student_rows[0]
    rows = x.shape[0]
    length = lax.dynamic_slice_in_dim(valid_length, me, 1)
    split = lax.dynamic_slice_in_dim(split_point, me, 1)

    def gather(weight, axis):
        return lax.all_gather(weight, "heads", axis=axis, tiled=True)

    w_five, b_five, w_out = gather(project_five, 2), gather(bias_five, 1), gather(output_five, 0)
    w_wide, b_wide, w_narrow = gather(widen_weight, 1), gather(widen_bias, 0), gather(narrow_weight, 0)
    w_six, b_six = gather(project_six, 2), gather(bias_six, 1)
    w_teacher, b_teacher = gather(teacher_project, 2), gather(teacher_bias, 1)

    positions = jnp.arange(rows, dtype=jnp.int32)[:, None]
    valid = positions < length
    counted_rows = valid & (positions != 0) & (positions != split - 1) & (positions != length - 1)
    row_weight = jnp.where(counted_rows, 1.0, 0.0).astype(f32) / (
        (length - 3).astype(f32) * float(all_seqs * HEADS)
    )

    q, k, v = project(x, w_five, b_five)
    weights, inverse, attended = attend_forward(length, q, k, v)
    x_wide = x.astype(f32)
    mixing = dot(attended, w_out) + branch_bias[0]
    middle, normed_one, rstd_one = norm_forward(x_wide + mixing, norm_gain[0], norm_bias[0])
    middle_low = middle.astype(bf16)
    pre_act = dot(middle_low, w_wide) + b_wide.astype(f32)
    activated, gelu_back = jax.vjp(exact_gelu, pre_act)
    activated = activated.astype(bf16)
    branch_two = dot(activated, w_narrow) + branch_bias[1]
    block, normed_two, rstd_two = norm_forward(middle + branch_two, norm_gain[1], norm_bias[1])
    block = block.astype(bf16)

    q6, k6, v6 = project(block, w_six, b_six)
    tq, tk, tv = project(teacher_rows[0], w_teacher, b_teacher)
    dq6, dk6, dv6, divergence = relations(length, q6, k6, v6, tq, tk, tv, row_weight)

    g6 = jnp.concatenate((dq6, dk6, dv6), axis=1)
    grad_six = dot(block.T, g6)
    flat_six = w_six.reshape(w_six.shape[0], -1)
    d_block = dot(g6, flat_six, NT)
    d_sum_two, gain_two, shift_two = norm_backward(d_block, normed_two, rstd_two, norm_gain[1])
    d_branch = d_sum_two.astype(bf16)
    grad_narrow = dot(activated.T, d_branch)
    d_pre = gelu_back(dot(d_branch, w_narrow, NT))[0].astype(bf16)
    grad_wide = dot(middle_low.T, d_pre)
    d_middle = d_sum_two + dot(d_pre, w_wide, NT)
    d_sum_one, gain_one, shift_one = norm_backward(d_middle, normed_one, rstd_one, norm_gain[0])
    d_mixing = d_sum_one.astype(bf16)
    grad_out = dot(attended.T, d_mixing)
    d_attended = dot(d_mixing, w_out, NT).astype(bf16)

    dq5, dk5, dv5 = attend_backward(q, k, v, weights, inverse, attended, d_attended)
    g5 = jnp.concatenate((dq5, dk5, dv5), axis=1)
    grad_five = dot(x.T, g5)
    flat_five = w_five.reshape(w_five.shape[0], -1)
    grad_in = d_sum_one + dot(g5, flat_five, NT)

    def by_share(grad, parts):
        r, width = grad.shape[0], grad.shape[1] // parts
        return jnp.transpose(grad.reshape(r, parts, shares, width // shares), (2, 0, 1, 3))

    (six,) = reduce_pieces([by_share(grad_six, 3)])
    wide, narrow, out = reduce_pieces(
        [
            by_share(grad_wide, 1)[:, :, 0],
            grad_narrow.reshape(shares, -1, D),
            grad_out.reshape(shares, -1, D),
        ]
    )
    (five,) = reduce_pieces([by_share(grad_five, 3)])

    def column_sums(grad):
        return jnp.sum(grad, axis=0, dtype=f32)

    kept = valid.astype(f32)
    partials = jnp.stack(
        (
            jnp.sum(divergence),
            jnp.sum(kept * x_wide * x_wide),
            jnp.sum(kept * mixing * mixing),
            jnp.sum(kept * branch_two * branch_two),
            jnp.sum(kept),
        )
    )
    vectors = (
        partials,
        jnp.stack((column_sums(d_mixing), column_sums(d_branch))),
        jnp.stack((gain_one, gain_two)),
        jnp.stack((shift_one, shift_two)),
        jnp.stack((column_sums(dq5), column_sums(dv5))),
        column_sums(d_pre)[None],
        jnp.stack((column_sums(dq6), column_sums(dv6))),
    )
    flat = lax.psum(jnp.concatenate([p.reshape(-1) for p in vectors]), ("heads", "batch"))
    summed = []
    offset = 0
    for p in vectors:
        summed.append(flat[offset : offset + p.size].reshape(p.shape))
        offset += p.size

    def own(grad):
        width = grad.shape[1] // shares
        return lax.dynamic_slice_in_dim(grad, me * width, width, axis=1)

    totals = summed[0]
    counted = totals[4] * D
    summary = jnp.stack(
        (
            totals[0],
            jnp.sqrt(totals[1] / counted),
            jnp.sqrt(totals[2] / counted),
            jnp.sqrt(totals[3] / counted),
        )
    )
    return (
        block[None], grad_in[None], five, own(summed[4]), out, summed[1], summed[2], summed[3],
        wide, own(summed[5])[0], narrow, six, own(summed[6]), summary,
    )


def solution(mesh):
    return jax.shard_map(
        body,
        mesh=mesh,
        in_specs=(
            P(("batch", "heads"), None, None),
            P(("batch", "heads"), None, None),
            P("batch"),
            P("batch"),
            P(None, None, "heads"),
            P(None, "heads"),
            P("heads", None),
            P(),
            P(),
            P(),
            P(None, "heads"),
            P("heads"),
            P("heads", None),
            P(None, None, "heads"),
            P(None, "heads"),
            P(None, None, "heads"),
            P(None, "heads"),
        ),
        out_specs=(
            P(("batch", "heads"), None, None),
            P(("batch", "heads"), None, None),
            P(None, None, "heads"),
            P(None, "heads"),
            P("heads", None),
            P(),
            P(),
            P(),
            P(None, "heads"),
            P("heads"),
            P("heads", None),
            P(None, None, "heads"),
            P(None, "heads"),
            P(),
        ),
        check_vma=False,
    )
```

time: 1700 us -> 985 us (0.58)
  waiting for transfers between devices: 748 us -> 308 us
  other arithmetic: 435 us -> 33.7 us
  matrix products: 322 us -> 74.7 us
  Pallas kernels: 0 us -> 220 us
  blocking collectives: 56.9 us -> 180 us
  local copies, waits for them, and re-layouts: 87.7 us -> 139 us
  loops' own time: 19.2 us -> 0 us
    all_gather x6 -> x3, waiting for transfers between devices: 421 us -> 0.02 us  [gather(): return lax.all_gather(weight, 'heads', axis=axis, tiled=True)]
    reduce_sum x53 -> x10, other arithmetic: 380 us -> 5.33 us  [the longest x6 2.99 us: column_sums(): return jnp.sum(grad, axis=0, dtype=f32)]
    unnamed x12 -> x11, waiting for transfers between devices: 1.38 us -> 308 us
    reduce_scatter x5 -> x0, waiting for transfers between devices: 285 us -> none  [the longest x1 109 us: body(): lax.psum_scatter(jnp.einsum('uor,re->uoe', attended_rows, fifth_output_we...]
    pallas_call x0 -> x3, Pallas kernels: none -> 220 us  [the longest x1 138 us: relations(): pl.pallas_call(relation_kernel, grid=(groups,), in_specs=[pl.BlockSpec(me...]
    all_gather x0 -> x10, blocking collectives: none -> 139 us  [the longest x7 109 us: gather(): return lax.all_gather(weight, 'heads', axis=axis, tiled=True)]
    sub x32 -> x0, matrix products: 131 us -> none  [log_softmax(): shifted = logits - highest]
    dot_general x104 -> x16, matrix products: 191 us -> 74.7 us  [dot(): return lax.dot_general(left, right, dims, preferred_element_type=f32)]
  transfers between devices with their start and end apart: 12 -> 7, of which waited for: 11 -> 4; matrix products, arithmetic and copies ran while one was open for 3% -> 17% of each run, Pallas kernels for 0% -> 4%
where the time goes in v1:
time: 985 us; the launch traced here: 976 us
  waiting for transfers between devices  308 us (31%)
  Pallas kernels  220 us (22%)
  blocking collectives  180 us (18%)
  local copies, waits for them, and re-layouts  139 us (14%)
  matrix products  74.7 us (8%)
  other arithmetic  33.7 us (3%)
  between operations  20.6 us (2%)
    unnamed x11, waiting for transfers between devices  308 us
    pallas_call x1, Pallas kernels, relations(): pl.pallas_call(relation_kernel, grid=(groups,), in_specs=[pl.BlockSpec(me...  138 us
    all_gather x7, blocking collectives, gather(): return lax.all_gather(weight, 'heads', axis=axis, tiled=True)  109 us
    unnamed x103, local copies, waits for them, and re-layouts  97.4 us
    dot_general x16, matrix products, dot(): return lax.dot_general(left, right, dims, preferred_element_type=f32)  74.7 us
    pallas_call x1, Pallas kernels, attend_forward(): pl.pallas_call(attend_forward_kernel, grid=(groups,), in_specs=[pl.BlockS...  41.6 us
    psum x1, blocking collectives, body(): lax.psum(jnp.concatenate([p.reshape(-1) for p in vectors]), ('heads', 'ba...  40.3 us
    pallas_call x1, Pallas kernels, attend_backward(): pl.pallas_call(attend_backward_kernel, grid=(groups,), in_specs=[wide, wi...  40.1 us
  transfers between devices with their start and end apart: 7, of which 4 were waited for; matrix products, arithmetic and copies ran while one was open for 17% of the time, Pallas kernels for 4%

profile of v1, /device:TPU:0, one launch (start us, length us, event | category | flops | bytes accessed | tf_op | source)
XLA Modules:
  0.0 975.5 jit_solution(1432449649471660585)
XLA Ops:
  10.8 1.4 convert_reduce_fusion.7
  19.2 12.7 %all-gather = bf16[4,96,2]{1,2,0:T(2,128)(2,1)S(1)} all-gather(bf16[1,96,2]{1,2,0:T(2,128)(2,1)} %bitcast.108), channel_id=1, replica_groups=mesh['heads'=4,'batch'=8] {'heads'}, dimensions={0}, use_global_device_ids=true | all-gather | bytes 1920 | tf_op jit(solution)/shard_map/all_gather | solution.py:334
  32.0 7.8 all-gather.2
  40.0 9.6 all-gather.3
  49.7 12.0 %all-gather.1 = bf16[4,1,384]{2,1,0:T(2,128)(2,1)S(1)} all-gather(bf16[1,1,384]{2,1,0:T(2,128)(2,1)S(1)} %reshape.262), channel_id=1, replica_groups=mesh['heads'=4,'batch'=8] {'heads'}, dimensions={0}, use_global_device_ids=true | all-gather | bytes 3840 | tf_op jit(solution)/shard_map/all_gather | solution.py:334
  61.8 16.5 %all_gather.41 = bf16[384,384]{1,0:T(8,128)(2,1)S(1)} all-gather(bf16[96,384]{1,0:T(8,128)(2,1)S(1)} %copy-done.27), channel_id=1, replica_groups=mesh['heads'=4,'batch'=8] {'heads'}, dimensions={0}, use_global_device_ids=true | all-gather | bytes 368640 | tf_op jit(solution)/shard_map/all_gather | solution.py:334
  79.5 21.1 %all_gather.39 = bf16[384,3,384]{0,2,1:T(8,128)(2,1)S(1)} all-gather(bf16[384,3,96]{0,2,1:T(8,128)(2,1)S(1)} %copy-done.25), channel_id=1, replica_groups=mesh['heads'=4,'batch'=8] {'heads'}, dimensions={2}, use_global_device_ids=true | all-gather | bytes 1105920 | tf_op jit(solution)/shard_map/all_gather | solution.py:334
  100.6 29.2 %all_gather.45 = bf16[384,3,384]{0,2,1:T(8,128)(2,1)} all-gather(bf16[384,3,96]{0,2,1:T(8,128)(2,1)S(1)} %copy-done.26), channel_id=1, replica_groups=mesh['heads'=4,'batch'=8] {'heads'}, dimensions={2}, use_global_device_ids=true | all-gather | bytes 1105920 | tf_op jit(solution)/shard_map/all_gather | solution.py:334
  129.8 1.5 fusion.19
  132.2 1.5 fusion.13
  133.7 41.6 %attend_forward.1 = (bf16[12,1024,1024]{2,1,0:T(8,128)(2,1)}, f32[1024,384]{1,0:T(8,128)}, bf16[1024,384]{1,0:T(8,128)(2,1)}) custom-call(s32[1]{0:T(128)} %dynamic_slice.13.length_ref, bf16[1024,384]{1,0:T(8,128)(2,1)} %get-tuple-element.118.q_ref, bf16[1024,384]{1,0:T(8,128)(2,1)} %slice.245.k_ref, bf16[1024,384]{1,0:T(8,128)(2,1)} %get-tuple-element.117.v_ref), custom_call_target="tpu_custom_call" | custom-call | tf_op jit(solution)/shard_map/attend_forward/pallas_call | solution.py:96
  175.3 2.9 fusion.40
  179.2 1.7 select_divide_fusion.w_ref
  180.9 18.7 %multiply_convert_fusion = (bf16[1024,1536]{1,0:T(8,128)(2,1)}, f32[1024,1536]{1,0:T(8,128)}, f32[1024,1536]{1,0:T(8,128)}) fusion(f32[1536]{0:T(1024)S(1)} %reshape.268, bf16[384,1536]{1,0:T(8,128)(2,1)} %all-gather.8.cloned.1.call-done, f32[1024,384]{0,1:T(8,128)S(1)} %get-tuple-element.112, f32[384]{0:T(512)S(1)} %get-tuple-element.93, ...), kind=kOutput, calls=%fused_computation.4 | convolution fusion | flops 1313734656 | bytes 18498560 | tf_op jit(solution)/shard_map/dot_general | solution.py:33
  199.7 6.2 fusion.10
  207.2 2.3 copy.67
  209.5 2.8 fusion.44
  213.3 1.4 fusion.11
  214.7 5.9 fusion.15
  220.6 1.3 slice.243.tk_ref
  221.9 2.4 fusion.6
  224.3 138.1 %relations.1 = (bf16[1024,384]{1,0:T(8,128)(2,1)}, bf16[1024,384]{1,0:T(8,128)(2,1)}, bf16[1024,384]{1,0:T(8,128)(2,1)}, f32[1024,1]{1,0:T(8,128)}) custom-call(s32[1]{0:T(128)} %dynamic_slice.13.length_ref, bf16[1024,384]{1,0:T(8,128)(2,1)} %get-tuple-element.116.q_ref, bf16[1024,384]{1,0:T(8,128)(2,1)} %slice.244.k_ref, ...), custom_call_target="tpu_custom_call" | custom-call | tf_op jit(solution)/shard_map/relations/pallas_call | solution.py:251
  362.4 1.3 constant_dynamic-update-slice_fusion.2
  365.0 2.6 fusion.43
  367.6 1.9 copy.60
  371.3 7.6 convert_reduce_fusion
  378.9 2.4 multiply_reduce_fusion.1
  383.1 1.6 convolution_convert_fusion.4.d_ref
  384.7 40.1 %attend_backward.1 = (bf16[1024,384]{1,0:T(8,128)(2,1)}, bf16[1024,384]{1,0:T(8,128)(2,1)}, bf16[1024,384]{1,0:T(8,128)(2,1)}) custom-call(bf16[1024,384]{1,0:T(8,128)(2,1)} %get-tuple-element.118.q_ref, bf16[1024,384]{1,0:T(8,128)(2,1)} %slice.245.k_ref, bf16[1024,384]{1,0:T(8,128)(2,1)} %get-tuple-element.117.v_ref, ...), custom_call_target="tpu_custom_call" | custom-call | tf_op jit(solution)/shard_map/attend_backward/pallas_call | solution.py:169
  424.8 1.3 constant_dynamic-update-slice_fusion.5
  427.3 2.4 convolution_convert_fusion.1
  429.7 3.4 copy.63
  433.2 19.5 %copy.80 = bf16[4,384,3,96]{0,3,2,1:T(8,128)(2,1)} copy(bf16[4,384,3,96]{3,2,1,0:T(4,128)(2,1)} %bitcast.94) | data formatting | bytes 1769472
  452.8 3.9 convolution_convert_fusion
  456.6 2.3 copy.65
  458.9 5.7 convolution_convert_fusion.2
  464.6 2.0 convert_element_type.203
  466.6 5.2 convolution_convert_fusion.3
  471.9 3.8 convert_element_type.199
  475.7 1.3 convolution_convert_fusion.5
  477.0 1.8 convert_element_type.205
  478.8 45.4 %copy.81 = bf16[4,384,3,96]{0,3,2,1:T(8,128)(2,1)} copy(bf16[4,384,3,96]{1,3,0,2:T(8,128)(2,1)} %bitcast.102) | data formatting | bytes 1769472
  524.3 13.3 %pad_maximum_fusion = bf16[4,331776]{1,0:T(4,128)(2,1)} fusion(bf16[4,36864]{1,0:T(4,128)(2,1)} %convert_element_type.205, bf16[4,147456]{1,0:T(4,128)(2,1)S(1)} %convert_element_type.203, bf16[4,147456]{1,0:T(4,128)(2,1)} %bitcast.95), kind=kLoop, calls=%fused_computation.27 | loop fusion | flops 7962624 | bytes 5308416 | tf_op jit(solution)/shard_map/concatenate | solution.py:303
  539.2 1.3 convert_reduce_fusion.4
  541.5 3.3 concatenate.14
  544.8 40.3 %psum.7 = f32[5381]{0:T(1024)S(1)} all-reduce(f32[5381]{0:T(1024)S(1)} %concatenate.14), channel_id=1, replica_groups=mesh['heads'=4,'batch'=8] {'heads','batch'}, use_global_device_ids=true, to_apply=%region_26.27 | all-reduce | flops 5381 | bytes 43048 | tf_op jit(solution)/shard_map/psum | solution.py:422
  590.4 38.2 %reduce-scatter.8.cloned.1.call-done = bf16[13824,4]{1,0:T(8,128)(2,1)} async-done(((bf16[110592,4]{1,0:T(8,128)(2,1)}), bf16[13824,4]{1,0:T(8,128)(2,1)}) %reduce-scatter.8.cloned.1.call-update) | async-done | bytes 110608
  628.6 4.0 copy.75
  632.6 172.8 %reduce-scatter.10.cloned.1.call-done = bf16[13824,4]{1,0:T(8,128)(2,1)} async-done(((bf16[110592,4]{1,0:T(8,128)(2,1)}), bf16[13824,4]{1,0:T(8,128)(2,1)}) %reduce-scatter.10.cloned.1.call-update) | async-done | bytes 110608
  805.5 4.1 copy.79
  809.5 64.2 %all-reduce.8.cloned.1.call-done = bf16[4,331776]{1,0:T(4,128)(2,1)} async-done(((bf16[4,331776]{1,0:T(4,128)(2,1)}), bf16[4,331776]{1,0:T(4,128)(2,1)}) %all-reduce.8.cloned.1.call-update) | async-done | bytes 2654224
  873.8 1.8 constant_dynamic-slice_fusion.2
  875.6 4.1 add_bitcast_fusion
  879.7 3.0 copy.68
  885.9 30.7 %all-reduce.10.cloned.1.call-done = (bf16[4,13824]{1,0:T(4,128)(2,1)}, bf16[4,41472]{1,0:T(4,128)(2,1)}, bf16[4,13824]{1,0:T(4,128)(2,1)}) async-done(((bf16[4,13824]{1,0:T(4,128)(2,1)}, bf16[4,41472]{1,0:T(4,128)(2,1)}, bf16[4,13824]{1,0:T(4,128)(2,1)}), (bf16[4,13824]{1,0:T(4,128)(2,1)}, bf16[4,41472]{1,0:T(4,128)(2,1)}, bf16[4,13824]{1,0:T(4,128)(2,1)})) %all-reduce.10.cloned.1.call-update) | async-done | bytes 552976
  916.6 1.7 constant_dynamic-slice_fusion.1
  918.3 12.0 %all_gather.50 = bf16[1,331776]{1,0:T(2,128)(2,1)S(1)} all-gather(bf16[1,41472]{1,0:T(2,128)(2,1)S(1)} %constant_dynamic-slice_fusion.1), channel_id=1, replica_groups=mesh['heads'=4,'batch'=8] {'batch'}, dimensions={1}, use_global_device_ids=true | all-gather | bytes 746496 | tf_op jit(solution)/shard_map/all_gather | solution.py:310
  930.3 1.6 convert_element_type.206
  933.0 6.2 slice_reduce_fusion
  940.5 9.1 all_gather.51
  949.5 1.2 convert_reduce_fusion.8
  952.4 9.4 all_gather.49
  961.8 1.2 convert_reduce_fusion.9
  965.7 1.6 slice.151
  (182 shorter events, 35.4 us)
Async XLA Ops:
  7.2 207.5 %copy-start = (bf16[1,1024,768]{2,1,0:T(8,128)(2,1)S(1)}, bf16[1,1024,768]{2,1,0:T(8,128)(2,1)}, u32[]{:S(2)}) copy-start(bf16[1,1024,768]{2,1,0:T(8,128)(2,1)} %param.18) | copy-start | bytes 4718596
  7.2 32.8 %copy-start.36 = (bf16[2,192]{1,0:T(2,128)(2,1)S(1)}, bf16[2,192]{1,0:T(2,128)(2,1)}, u32[]{:S(2)}) copy-start(bf16[2,192]{1,0:T(2,128)(2,1)} %param.33) | copy-start | bytes 2308
  7.2 42.5 %copy-start.31 = (f32[2,384]{1,0:T(2,128)S(1)}, f32[2,384]{1,0:T(2,128)}, u32[]{:S(2)}) copy-start(f32[2,384]{1,0:T(2,128)} %param.24) | copy-start | bytes 9220
  7.2 54.5 %copy-start.27 = (bf16[96,384]{1,0:T(8,128)(2,1)S(1)}, bf16[96,384]{1,0:T(8,128)(2,1)}, u32[]{:S(2)}) copy-start(bf16[96,384]{1,0:T(8,128)(2,1)} %param.23) | copy-start | bytes 221188
  7.2 71.1 %copy-start.7 = (bf16[1,1024,384]{2,1,0:T(8,128)(2,1)S(1)}, bf16[1,1024,384]{2,1,0:T(8,128)(2,1)}, u32[]{:S(2)}) copy-start(bf16[1,1024,384]{2,1,0:T(8,128)(2,1)} %param.17) | copy-start | bytes 2359300
  7.2 173.7 %all-gather.8.cloned.1.call-start = ((), (), s32[]{:S(2)}) async-start(), calls=%async_computation.2 | async-start | bytes 1474560 | tf_op jit(solution)/shard_map/all_gather | solution.py:334
  8.0 191.7 %all-gather.10.cloned.1.call-start = ((), (), s32[]{:S(2)}) async-start(), calls=%async_computation.3 | async-start | bytes 1474560 | tf_op jit(solution)/shard_map/all_gather | solution.py:334
  8.7 70.7 %copy-start.25 = (bf16[384,3,96]{0,2,1:T(8,128)(2,1)S(1)}, bf16[384,3,96]{0,2,1:T(8,128)(2,1)}, u32[]{:S(2)}) copy-start(bf16[384,3,96]{0,2,1:T(8,128)(2,1)} %param.21) | copy-start | bytes 663556
  8.7 206.0 %all-gather.12.cloned.1.call-start = ((), (), s32[]{:S(2)}) async-start(), calls=%async_computation.4 | async-start | bytes 4423680 | tf_op jit(solution)/shard_map/all_gather | solution.py:334
  9.5 619.1 %reduce-scatter.8.cloned.1.call-start = ((), (), s32[]{:S(2)}) async-start(), calls=%async_computation.5 | async-start | bytes 31850496
  39.9 60.7 %copy-start.26 = (bf16[384,3,96]{0,2,1:T(8,128)(2,1)S(1)}, bf16[384,3,96]{0,2,1:T(8,128)(2,1)}, u32[]{:S(2)}) copy-start(bf16[384,3,96]{0,2,1:T(8,128)(2,1)} %param.30) | copy-start | bytes 663556
  100.6 30.6 %copy-start.9 = (bf16[384,3,384]{0,2,1:T(8,128)(2,1)}, bf16[384,3,384]{0,2,1:T(8,128)(2,1)S(1)}, u32[]{:S(2)}) copy-start(bf16[384,3,384]{0,2,1:T(8,128)(2,1)S(1)} %all_gather.39) | copy-start | bytes 2654212
  133.7 41.6 %copy-start.17 = (bf16[1,1024,384]{1,2,0:T(8,128)(2,1)S(1)}, bf16[1,1024,384]{1,2,0:T(8,128)(2,1)}, u32[]{:S(2)}) copy-start(bf16[1,1024,384]{1,2,0:T(8,128)(2,1)} %copy.55) | copy-start | bytes 2359300
  178.3 21.4 %copy-start.2 = (f32[1024,384]{0,1:T(8,128)}, f32[1024,384]{0,1:T(8,128)S(1)}, u32[]{:S(2)}) copy-start(f32[1024,384]{0,1:T(8,128)S(1)} %get-tuple-element.112) | copy-start | bytes 4718596
  178.3 0.9 copy-start.32
  178.3 0.9 copy-start.33
  362.4 1.4 copy-start.20
  362.4 1.6 copy-start.12
  363.8 1.2 copy-start.11
  365.0 2.6 copy-start.23
  370.0 1.3 copy-start.38
  370.6 8.3 copy-start.18
  371.3 7.6 copy-start.3
  371.3 7.6 copy-start.37
  378.9 2.4 copy-start.39
  382.0 1.1 copy-start.4
  424.8 1.4 copy-start.21
  424.8 1.6 copy-start.15
  426.2 1.2 copy-start.8
  427.3 2.4 copy-start.24
  452.7 352.7 %reduce-scatter.10.cloned.1.call-start = ((), (), s32[]{:S(2)}) async-start(), calls=%async_computation.6 | async-start | bytes 31850496
  456.6 2.3 copy-start.19
  471.9 3.8 copy-start.5
  471.9 3.8 copy-start.6
  524.2 349.6 %all-reduce.8.cloned.1.call-start = ((), (), s32[]{:S(2)}) async-start(), calls=%async_computation.7 | async-start | bytes 5308416
  524.3 13.3 %copy-start.14 = (bf16[1024,384]{1,0:T(8,128)(2,1)S(1)}, bf16[1024,384]{1,0:T(8,128)(2,1)}, u32[]{:S(2)}) copy-start(bf16[1024,384]{1,0:T(8,128)(2,1)} %get-tuple-element.25) | copy-start | bytes 2359300
  537.6 1.3 copy-start.13
  537.8 1.3 copy-start.35
  537.8 1.4 copy-start.34
  537.8 2.8 copy-start.16
  537.8 3.7 copy-start.30
  537.8 378.8 %all-reduce.10.cloned.1.call-start = ((), (), s32[]{:S(2)}) async-start(), calls=%async_computation.8 | async-start | bytes 1105920
  539.0 1.7 copy-start.22
  805.4 70.2 %copy-start.10 = (bf16[384,3,384]{0,2,1:T(8,128)(2,1)S(1)}, bf16[384,3,384]{0,2,1:T(8,128)(2,1)}, u32[]{:S(2)}) copy-start(bf16[384,3,384]{0,2,1:T(8,128)(2,1)} %copy-done.9) | copy-start | bytes 2654212
  932.0 7.2 copy-start.29
  932.0 7.9 copy-start.28
  963.7 4.5 copy-start.1
Sparse Core Ops, SparseCore 0:
  9.7 32.8 all-gather.7
  44.2 37.8 all-gather.9
  83.7 83.0 all-gather.11
  452.8 175.7 reduce-scatter.7
  632.2 173.2 reduce-scatter.9
  808.6 65.1 all-reduce.7
  877.7 38.8 all-reduce.9

commit v2 on v1

v2 whole, which is shorter than its diff:
```python
import functools
import math

import jax
import jax.numpy as jnp
from jax import lax
from jax.experimental import pallas as pl
from jax.experimental.pallas import tpu as pltpu
from jax.sharding import PartitionSpec as P

D = 384
HEADS = 12
HEAD_DIM = 32
TEACHER_HEAD_DIM = 64
PART = 3
TILE = 256
STRIP = 16
NORM_EPS = 1e-12
MASKED = -1e30
SAFE = 64.0
LN2 = math.log(2.0)
STUDENT_SCALE = 1.0 / math.sqrt(HEAD_DIM)
STUDENT_LOG = math.log2(math.e) / math.sqrt(HEAD_DIM)
TEACHER_LOG = math.log2(math.e) / math.sqrt(TEACHER_HEAD_DIM)
VMEM = 56 * 2**20

f32 = jnp.float32
bf16 = jnp.bfloat16

NN = (((1,), (0,)), ((), ()))
NT = (((1,), (1,)), ((), ()))
TN = (((0,), (0,)), ((), ()))


def dot(left, right, dims=NN):
    return lax.dot_general(left, right, dims, preferred_element_type=f32)


def lanes(shape):
    return lax.broadcasted_iota(jnp.int32, shape, 1)


def wide_rows(rows):
    return jnp.concatenate([rows, jnp.zeros((rows.shape[0], 128 - rows.shape[1]), rows.dtype)], axis=1)


def in_head(lane, head, size=HEAD_DIM):
    return (lane >= head * size) & (lane < (head + 1) * size)


def split_terms(rows, head, size, extra):
    inside = in_head(lanes(rows.shape), head, size)
    high = rows.astype(bf16).astype(f32)
    first = jnp.where(inside, high, extra).astype(bf16)
    second = jnp.where(inside, rows - high, 0.0).astype(bf16)
    return jnp.concatenate([first, second], axis=1)


def key_bias(rows, length):
    position = lax.broadcasted_iota(jnp.int32, (rows, 1), 0)
    return jnp.where(position < length, 0.0, MASKED)


def fold(tile, combine):
    total = tile[:, :128]
    for column in range(128, tile.shape[1], 128):
        total = combine(total, tile[:, column : column + 128])
    return total


def row_sum(tile):
    return jnp.sum(fold(tile, jnp.add), axis=1, keepdims=True)


def weave(first, second):
    done = 0
    for index, step in enumerate(second):
        while done < len(first) and done * len(second) < len(first) * (index + 1):
            first[done]()
            done += 1
        step()
    for step in first[done:]:
        step()


def step_place(step, tile, per_head):
    head = step // per_head
    return head, pl.ds(pl.multiple_of(lax.rem(step, per_head) * tile, tile), tile)


def run_pipeline(steps, logits, vector, back, enter=None):
    def stage(step, slot, before, after):
        if enter is not None:
            enter(step)
        ahead = logits(step + 1, 1 - slot) if after else []
        behind = back(step - 1, 1 - slot) if before else []
        weave(ahead + behind, vector(step, slot))

    for chunk in logits(jnp.int32(0), 0):
        chunk()
    stage(jnp.int32(0), 0, False, True)

    def pair(index, carry):
        stage(2 * index + 1, 1, True, True)
        stage(2 * index + 2, 0, True, True)
        return carry

    lax.fori_loop(0, (steps - 2) // 2, pair, 0)
    stage(jnp.int32(steps - 1), 1, True, False)
    for chunk in back(jnp.int32(steps - 1), 1):
        chunk()


def project_part(x, w_ref, index, bias):
    flat = dot(x, w_ref[index * 96 : (index + 1) * 96, :], NT)
    if bias is not None:
        flat = flat + bias
    return wide_rows(flat).astype(bf16)


def attend_forward_kernel(
    length_ref, x_ref, w_ref, b_ref, q_ref, k_ref, v_ref, e_hbm, r_ref, o_ref, lhs, rhs, mixer, zs, e_all, sems
):
    rows = x_ref.shape[0]
    tile = min(TILE, rows)
    per_head = rows // tile
    steps = PART * per_head
    x = x_ref[...]
    q = project_part(x, w_ref, 0, b_ref[0:1, :96])
    k = project_part(x, w_ref, 1, None)
    v = project_part(x, w_ref, 2, b_ref[1:2, :96])
    q_ref[...] = q
    k_ref[...] = k
    v_ref[...] = v
    lane = lanes((rows, 128))
    one = jnp.where(lane == 96, 1.0, 0.0)
    for head in range(PART):
        lhs[head] = jnp.where(in_head(lane, head), q.astype(f32), one).astype(bf16)
    rhs[...] = jnp.where(lane == 96, key_bias(rows, length_ref[0]), k.astype(f32)).astype(bf16)
    mixer[...] = jnp.where(lane == 96, 1.0, v.astype(f32)).astype(bf16)
    o_ref[...] = jnp.zeros_like(o_ref)
    r_ref[...] = jnp.zeros_like(r_ref)

    def out_copy(step):
        head, span = step_place(step, tile, per_head)
        return pltpu.make_async_copy(e_all.at[head, span], e_hbm.at[head, span], sems.at[step])

    def logits(step, slot):
        head, span = step_place(step, tile, per_head)

        def chunk(start):
            zs[slot, :, start : start + 256] = dot(lhs[head, span, :], rhs[start : start + 256, :], NT)

        return [functools.partial(chunk, start) for start in range(0, rows, 256)]

    def vector(step, slot):
        head, span = step_place(step, tile, per_head)
        base = lax.rem(step, per_head) * tile

        def strip(start):
            z = zs[slot, start : start + STRIP, :]
            highest = jnp.max(fold(z, jnp.maximum), axis=1, keepdims=True)
            here = pl.ds(pl.multiple_of(base + start, STRIP), STRIP)
            e_all[head, here, :] = jnp.exp2((z - highest) * STUDENT_LOG).astype(bf16)

        return [functools.partial(strip, start) for start in range(0, tile, STRIP)]

    def back(step, slot):
        head, span = step_place(step, tile, per_head)

        def mix():
            mixed = dot(e_all[head, span, :], mixer[...])
            inverse = 1.0 / mixed[:, 96:97]
            inside = in_head(lanes(mixed.shape), head)
            o_ref[span, :] = jnp.where(inside, mixed * inverse, o_ref[span, :].astype(f32)).astype(bf16)
            r_ref[span, :] = jnp.where(inside, inverse, r_ref[span, :])

        return [mix]

    def enter(step):
        @pl.when(step > 0)
        def _():
            out_copy(step - 1).start()

    run_pipeline(steps, logits, vector, back, enter)
    out_copy(jnp.int32(steps - 1)).start()

    def finish(step, carry):
        out_copy(step).wait()
        return carry

    lax.fori_loop(0, steps, finish, 0)


def whole(shape):
    return pl.BlockSpec(shape, lambda *_: (0,) * len(shape))


SMEM = pl.BlockSpec(memory_space=pltpu.SMEM)
ANY = pl.BlockSpec(memory_space=pl.ANY)


def cost(micros):
    return pl.CostEstimate(flops=int(micros * 1.1e9), bytes_accessed=1024, transcendentals=0)


def attend_forward(length, x, w, b):
    rows = x.shape[0]
    narrow = jax.ShapeDtypeStruct((rows, 128), bf16)
    steps = PART * (rows // min(TILE, rows))
    return pl.pallas_call(
        attend_forward_kernel,
        grid=(1,),
        in_specs=[SMEM, whole(x.shape), whole(w.shape), whole(b.shape)],
        out_specs=[whole((rows, 128))] * 3 + [ANY] + [whole((rows, 128))] * 2,
        out_shape=[
            narrow, narrow, narrow, jax.ShapeDtypeStruct((PART, rows, rows), bf16),
            jax.ShapeDtypeStruct((rows, 128), f32), narrow,
        ],
        scratch_shapes=[
            pltpu.VMEM((PART, rows, 128), bf16),
            pltpu.VMEM((rows, 128), bf16),
            pltpu.VMEM((rows, 128), bf16),
            pltpu.VMEM((2, min(TILE, rows), rows), f32),
            pltpu.VMEM((PART, rows, rows), bf16),
            pltpu.SemaphoreType.DMA((steps,)),
        ],
        compiler_params=pltpu.CompilerParams(vmem_limit_bytes=VMEM),
        cost_estimate=cost(9),
        name="attend_forward",
    )(length, x, w, b)


def attend_backward_kernel(
    q_ref, k_ref, v_ref, e_hbm, r_ref, a_ref, d_ref, x_ref, w_ref, acc_ref, g_ref, in_ref,
    lhs, rhs, keys, qt, dt, zs, gs, dq, dkt, dvt, e_all, sems,
):
    rows = q_ref.shape[0]
    tile = min(TILE, rows)
    per_head = rows // tile
    steps = PART * per_head

    def in_copy(step):
        head, span = step_place(step, tile, per_head)
        return pltpu.make_async_copy(e_hbm.at[head, span], e_all.at[head, span], sems.at[step])

    def begin(step, carry):
        in_copy(step).start()
        return carry

    lax.fori_loop(0, steps, begin, 0)
    lane = lanes((rows, 128))
    grads = r_ref[...] * d_ref[...].astype(f32)
    shifts = grads * a_ref[...].astype(f32)
    k = k_ref[...].astype(f32)
    for head in range(PART):
        inside = in_head(lane, head)
        shift = -jnp.sum(jnp.where(inside, shifts, 0.0), axis=1, keepdims=True)
        high = shift.astype(bf16).astype(f32)
        lhs[head] = split_terms(
            grads, head, HEAD_DIM, jnp.where(lane == 96, high, jnp.where(lane == 97, shift - high, 0.0))
        )
        keys[head] = jnp.where(inside, k, 0.0).astype(bf16)
    rhs[:, :128] = jnp.where((lane == 96) | (lane == 97), 1.0, v_ref[...].astype(f32)).astype(bf16)
    rhs[:, 128:] = v_ref[...]
    qt[...] = q_ref[...].T
    dt[...] = grads.astype(bf16).T
    dq[...] = jnp.zeros_like(dq)
    dkt[...] = jnp.zeros_like(dkt)
    dvt[...] = jnp.zeros_like(dvt)

    def logits(step, slot):
        head, span = step_place(step, tile, per_head)

        def chunk(start):
            zs[slot, :, start : start + 256] = dot(lhs[head, span, :], rhs[start : start + 256, :], NT)

        return [functools.partial(chunk, start) for start in range(0, rows, 256)]

    def vector(step, slot):
        head, span = step_place(step, tile, per_head)
        base = lax.rem(step, per_head) * tile

        def strip(start):
            here = pl.ds(pl.multiple_of(base + start, STRIP), STRIP)
            weights = e_all[head, here, :].astype(f32)
            gs[slot, start : start + STRIP, :] = (weights * zs[slot, start : start + STRIP, :]).astype(bf16)

        return [functools.partial(strip, start) for start in range(0, tile, STRIP)]

    def back(step, slot):
        head, span = step_place(step, tile, per_head)
        own = pl.ds(pl.multiple_of(head * HEAD_DIM, HEAD_DIM), HEAD_DIM)

        def first():
            dq[span, :] += dot(gs[slot], keys[head])

        def second(start):
            part = slice(start, start + 256)
            dkt[own, part] += dot(qt[own, span], gs[slot, :, part])

        def third(start):
            part = slice(start, start + 256)
            dvt[own, part] += dot(dt[own, span], e_all[head, span, part])

        starts = range(0, rows, 256)
        return [first] + [functools.partial(second, s) for s in starts] + [functools.partial(third, s) for s in starts]

    run_pipeline(steps, logits, vector, back, lambda step: in_copy(step).wait())
    grads = (
        (dq[...] * STUDENT_SCALE).astype(bf16),
        (dkt[...] * STUDENT_SCALE).T.astype(bf16),
        dvt[...].T.astype(bf16),
    )
    weight_grads(grads, x_ref[...], g_ref)
    in_ref[...] = acc_ref[...] + spread(grads, w_ref)


def weight_grads(grads, x, g_ref):
    for index, grad in enumerate(grads):
        g_ref[index * 96 : (index + 1) * 96, :] = dot(grad, x, TN)[:96].astype(bf16)
    ones = jnp.ones((8, x.shape[0]), bf16)
    row = lax.broadcasted_iota(jnp.int32, (8, 128), 0)
    sums = jnp.where(row == 0, dot(ones, grads[0]), jnp.where(row == 1, dot(ones, grads[2]), 0.0))
    sums = jnp.concatenate([sums, jnp.zeros((8, x.shape[1] - 128), f32)], axis=1)
    g_ref[288:304, :] = jnp.concatenate([sums, jnp.zeros_like(sums)], axis=0).astype(bf16)


def spread(grads, w_ref):
    total = None
    for index, grad in enumerate(grads):
        term = dot(grad[:, :96], w_ref[index * 96 : (index + 1) * 96, :])
        total = term if total is None else total + term
    return total


def attend_backward(q, k, v, e, r, attended, d_attended, x, w, grad_in):
    rows = x.shape[0]
    tile = min(TILE, rows)
    row = whole((rows, 128))
    return pl.pallas_call(
        attend_backward_kernel,
        grid=(1,),
        in_specs=[row, row, row, ANY, row, row, row, whole(x.shape), whole(w.shape), whole(x.shape)],
        out_specs=[whole((304, x.shape[1])), whole(x.shape)],
        out_shape=[jax.ShapeDtypeStruct((304, x.shape[1]), bf16), jax.ShapeDtypeStruct(x.shape, f32)],
        scratch_shapes=[
            pltpu.VMEM((PART, rows, 256), bf16),
            pltpu.VMEM((rows, 256), bf16),
            pltpu.VMEM((PART, rows, 128), bf16),
            pltpu.VMEM((128, rows), bf16),
            pltpu.VMEM((128, rows), bf16),
            pltpu.VMEM((2, tile, rows), f32),
            pltpu.VMEM((2, tile, rows), bf16),
            pltpu.VMEM((rows, 128), f32),
            pltpu.VMEM((128, rows), f32),
            pltpu.VMEM((128, rows), f32),
            pltpu.VMEM((PART, rows, rows), bf16),
            pltpu.SemaphoreType.DMA((PART * (rows // tile),)),
        ],
        compiler_params=pltpu.CompilerParams(vmem_limit_bytes=VMEM),
        cost_estimate=cost(10),
        name="attend_backward",
    )(q, k, v, e, r, attended, d_attended, x, w, grad_in)


def relation_kernel(
    numbers, block_ref, teacher_ref, w_ref, b_ref, tw_ref, tb_ref, d_ref, g_ref, kl_ref,
    ls, rs, lt, rt, keys, left_t, zs, zt, gs, left_sum, right_t, es_all, et_all, weight, grads_s, *, all_rows,
):
    rows = block_ref.shape[0]
    tile = min(TILE, rows)
    per_head = rows // tile
    steps = PART * per_head
    length, split = numbers[0], numbers[1]
    block = block_ref[...]
    teacher = teacher_ref[...]
    w_ref, b_ref, tw_ref, tb_ref, g_ref = (r.at[0] for r in (w_ref, b_ref, tw_ref, tb_ref, g_ref))
    lane = lanes((rows, 128))
    position = lax.broadcasted_iota(jnp.int32, (rows, 1), 0)
    bias = key_bias(rows, length)

    @pl.when(pl.program_id(0) == 0)
    def _():
        counted = (position < length) & (position != 0) & (position != split - 1) & (position != length - 1)
        share = 1.0 / ((length - 3).astype(f32) * float(all_rows))
        weight[...] = jnp.where(counted, share, 0.0)
        kl_ref[...] = jnp.zeros_like(kl_ref)
        d_ref[...] = jnp.zeros_like(d_ref)

    def teacher_part(index, b):
        flat = dot(teacher, tw_ref[index * 192 : (index + 1) * 192, :], NT)
        if b is not None:
            flat = flat + b
        flat = flat.astype(bf16)
        return flat[:, :128], wide_rows(flat[:, 128:])

    def largest(rows_low, size, blocks):
        square = rows_low.astype(f32)
        square = (square * square).astype(bf16)
        feature = lax.broadcasted_iota(jnp.int32, (128, 128), 0) // size
        same = feature == lanes((128, 128)) // size
        return jnp.max(dot(square, jnp.where(same, 1.0, 0.0).astype(bf16)), axis=0, keepdims=True)

    def relate(left, right, t_left, t_right, symmetric):
        left_sum[...] = jnp.zeros_like(left_sum)
        right_t[...] = jnp.zeros_like(right_t)
        left_t[...] = left.T
        left_wide = left.astype(f32) * STUDENT_LOG
        right_wide = right.astype(f32)
        one = jnp.where(lane == 96, 1.0, 0.0)
        if symmetric:
            one = jnp.where(lane == 97, bias, one)
        first = jnp.where(lane == 96, bias, right_wide)
        if symmetric:
            first = jnp.where(lane == 97, 1.0, first)
        rs[:, :128] = first.astype(bf16)
        rs[:, 128:] = right
        for head in range(PART):
            ls[head] = split_terms(left_wide, head, HEAD_DIM, one)
            keys[head] = jnp.where(in_head(lane, head), right_wide, 0.0).astype(bf16)
            own = head % 2
            spare = (1 - own) * TEACHER_HEAD_DIM
            one_t = jnp.where(lane == spare, 1.0, 0.0)
            wide_t = t_right[head // 2].astype(f32)
            first_t = jnp.where(lane == spare, bias, wide_t)
            if symmetric:
                one_t = jnp.where(lane == spare + 1, bias, one_t)
                first_t = jnp.where(lane == spare + 1, 1.0, first_t)
            lt[head] = split_terms(t_left[head // 2].astype(f32) * TEACHER_LOG, own, TEACHER_HEAD_DIM, one_t)
            rt[head, :, :128] = first_t.astype(bf16)
            rt[head, :, 128:] = t_right[head // 2]
        student_bound = largest(left, HEAD_DIM, 4) * largest(right, HEAD_DIM, 4) * STUDENT_LOG**2
        bound = jnp.max(student_bound)
        for part in range(2):
            t_bound = largest(t_left[part], TEACHER_HEAD_DIM, 2) * largest(t_right[part], TEACHER_HEAD_DIM, 2)
            bound = jnp.maximum(bound, jnp.max(t_bound * TEACHER_LOG**2))
        near = bound < SAFE * SAFE

        @pl.when(near)
        def _():
            if symmetric:
                symmetric_pass()
            else:
                plain_pass()

        @pl.when(jnp.logical_not(near))
        def _():
            for head in range(PART):
                own = head % 2
                spare = (1 - own) * TEACHER_HEAD_DIM
                ls[head] = split_terms(left.astype(f32), head, HEAD_DIM, jnp.where(lane == 96, 1.0, 0.0))
                lt[head] = split_terms(
                    t_left[head // 2].astype(f32), own, TEACHER_HEAD_DIM, jnp.where(lane == spare, 1.0, 0.0)
                )
            shifted_pass()

    def plain_pass():
        def logits(step, slot):
            head, span = step_place(step, tile, per_head)

            def student(start):
                zs[slot, :, start : start + 256] = dot(ls[head, span, :], rs[start : start + 256, :], NT)

            def taught(start):
                zt[slot, :, start : start + 256] = dot(lt[head, span, :], rt[head, start : start + 256, :], NT)

            chunks = []
            for start in range(0, rows, 256):
                chunks += [functools.partial(student, start), functools.partial(taught, start)]
            return chunks

        def vector(step, slot):
            base = lax.rem(step, per_head) * tile

            def strip(start):
                here = pl.ds(pl.multiple_of(base + start, STRIP), STRIP)
                student = zs[slot, start : start + STRIP, :]
                taught = zt[slot, start : start + STRIP, :]
                es = jnp.exp2(student)
                et = jnp.exp2(taught)
                sum_s = row_sum(es)
                sum_t = row_sum(et)
                cross = row_sum(et * (taught - student))
                w = weight[here, :]
                inverse = 1.0 / sum_t
                kl_ref[here, :] += w * (LN2 * cross * inverse + jnp.log(sum_s) - jnp.log(sum_t))
                gs[slot, start : start + STRIP, :] = (es * (w / sum_s) - et * (w * inverse)).astype(bf16)

            return [functools.partial(strip, start) for start in range(0, tile, STRIP)]

        run_pipeline(steps, logits, vector, grad_products)

    def grad_products(step, slot):
        head, span = step_place(step, tile, per_head)
        own = pl.ds(pl.multiple_of(head * HEAD_DIM, HEAD_DIM), HEAD_DIM)

        def first():
            left_sum[span, :] += dot(gs[slot], keys[head])

        def second(start):
            part = slice(start, start + 256)
            right_t[own, part] += dot(left_t[own, span], gs[slot, :, part])

        return [first] + [functools.partial(second, start) for start in range(0, rows, 256)]

    def shifted_pass():
        def one(step, carry):
            head, span = step_place(step, tile, per_head)
            student = dot(ls[head, span, :], rs[...], NT)
            student = (student - jnp.max(student, axis=1, keepdims=True)) * STUDENT_LOG
            taught = dot(lt[head, span, :], rt[head], NT)
            taught = (taught - jnp.max(taught, axis=1, keepdims=True)) * TEACHER_LOG
            es = jnp.exp2(student)
            et = jnp.exp2(taught)
            sum_s = jnp.sum(es, axis=1, keepdims=True)
            sum_t = jnp.sum(et, axis=1, keepdims=True)
            cross = jnp.sum(et * (taught - student), axis=1, keepdims=True)
            w = weight[span, :]
            row = LN2 * cross / sum_t + jnp.log(sum_s) - jnp.log(sum_t)
            kl_ref[span, :] += jnp.where(w > 0.0, w * row, 0.0)
            gs[0] = (es * (w / sum_s) - et * (w / sum_t)).astype(bf16)
            for chunk in grad_products(step, 0):
                chunk()
            return carry

        lax.fori_loop(0, steps, one, 0)

    def symmetric_pass():
        size = tile
        count = rows // size

        def column(row):
            return jnp.broadcast_to(row, (128, size)).T[:, :1]

        def row_of(value):
            return jnp.broadcast_to(value, (size, 128)).T[:1, :]

        def one_head(head, carry):
            own = pl.ds(pl.multiple_of(head * HEAD_DIM, HEAD_DIM), HEAD_DIM)
            by_row = []
            by_column = [[jnp.zeros((1, size), f32)] * 3 for _ in range(count)]
            for i in range(count):
                here = slice(i * size, (i + 1) * size)
                after = slice(i * size, rows)
                student = dot(ls[head, here, :], rs[after, :], NT)
                taught = dot(lt[head, here, :], rt[head, after, :], NT)
                es = jnp.exp2(student)
                et = jnp.exp2(taught)
                cross = et * (taught - student)
                es_all[here, after] = es
                et_all[here, after] = et
                by_row.append([row_sum(t) for t in (es, et, cross)])
                for j in range(i + 1, count):
                    part = slice((j - i) * size, (j - i + 1) * size)
                    by_column[j] = [
                        c + jnp.sum(t[:, part], axis=0, keepdims=True)
                        for c, t in zip(by_column[j], (es, et, cross))
                    ]
            a, b = [], []
            for i in range(count):
                here = slice(i * size, (i + 1) * size)
                sum_s, sum_t, cross = (r + column(c) for r, c in zip(by_row[i], by_column[i]))
                w = weight[here, :]
                sum_s = jnp.where(w > 0.0, sum_s, 1.0)
                sum_t = jnp.where(w > 0.0, sum_t, 1.0)
                inverse = 1.0 / sum_t
                kl_ref[here, :] += w * (LN2 * cross * inverse + jnp.log(sum_s) - jnp.log(sum_t))
                a.append(w / sum_s)
                b.append(w * inverse)
            a_row = jnp.concatenate([row_of(t) for t in a], axis=1)
            b_row = jnp.concatenate([row_of(t) for t in b], axis=1)
            for i in range(count):
                here = slice(i * size, (i + 1) * size)
                after = slice(i * size, rows)
                both = es_all[here, after] * (a[i] + a_row[:, after])
                both = (both - et_all[here, after] * (b[i] + b_row[:, after])).astype(bf16)
                left_sum[here, :] += dot(both, keys[head, after, :])
                if i + 1 < count:
                    right_t[own, (i + 1) * size :] += dot(left_t[own, here], both[:, size:])
            return carry

        lax.fori_loop(0, PART, one_head, 0)

    q = project_part(block, w_ref, 0, b_ref[0:1, :96])
    k = project_part(block, w_ref, 1, None)
    tq = teacher_part(0, tb_ref[0:1, :192])
    tk = teacher_part(1, None)
    relate(q, k, tq, tk, False)
    grads_s[0] = (left_sum[...] * STUDENT_SCALE).astype(bf16)
    grads_s[1] = (right_t[...] * STUDENT_SCALE).T.astype(bf16)
    v = project_part(block, w_ref, 2, b_ref[1:2, :96])
    tv = teacher_part(2, tb_ref[1:2, :192])
    relate(v, v, tv, tv, True)
    grads_s[2] = ((left_sum[...] + right_t[...].T) * STUDENT_SCALE).astype(bf16)
    grads = tuple(grads_s[i] for i in range(3))
    weight_grads(grads, block, g_ref)
    d_ref[...] += spread(grads, w_ref)


def relations(numbers, block, teacher, w, b, tw, tb, all_rows):
    rows = block.shape[0]
    tile = min(TILE, rows)
    shares = w.shape[0]

    def share(shape):
        return pl.BlockSpec((1,) + shape[1:], lambda s: (s,) + (0,) * (len(shape) - 1))

    return pl.pallas_call(
        functools.partial(relation_kernel, all_rows=all_rows),
        grid=(shares,),
        in_specs=[
            SMEM, whole(block.shape), whole(teacher.shape), share(w.shape), share(b.shape), share(tw.shape),
            share(tb.shape),
        ],
        out_specs=[whole(block.shape), share((shares, 304, D)), whole((rows, 1))],
        out_shape=[
            jax.ShapeDtypeStruct(block.shape, f32),
            jax.ShapeDtypeStruct((shares, 304, D), bf16),
            jax.ShapeDtypeStruct((rows, 1), f32),
        ],
        scratch_shapes=[
            pltpu.VMEM((PART, rows, 256), bf16),
            pltpu.VMEM((rows, 256), bf16),
            pltpu.VMEM((PART, rows, 256), bf16),
            pltpu.VMEM((PART, rows, 256), bf16),
            pltpu.VMEM((PART, rows, 128), bf16),
            pltpu.VMEM((128, rows), bf16),
            pltpu.VMEM((2, tile, rows), f32),
            pltpu.VMEM((2, tile, rows), f32),
            pltpu.VMEM((2, tile, rows), bf16),
            pltpu.VMEM((rows, 128), f32),
            pltpu.VMEM((128, rows), f32),
            pltpu.VMEM((rows, rows), f32),
            pltpu.VMEM((rows, rows), f32),
            pltpu.VMEM((rows, 1), f32),
            pltpu.VMEM((3, rows, 128), bf16),
        ],
        compiler_params=pltpu.CompilerParams(vmem_limit_bytes=VMEM),
        cost_estimate=cost(110),
        name="relations",
    )(numbers, block, teacher, w, b, tw, tb)


def norm_forward(rows, gain, shift):
    center = jnp.mean(rows, axis=1, keepdims=True)
    offsets = rows - center
    rstd = lax.rsqrt(jnp.mean(offsets * offsets, axis=1, keepdims=True) + NORM_EPS)
    normed = offsets * rstd
    return normed * gain + shift, normed, rstd


def norm_backward(grad, normed, rstd, gain):
    inner = grad * gain
    mean = jnp.mean(inner, axis=1, keepdims=True)
    slope = jnp.mean(inner * normed, axis=1, keepdims=True)
    return rstd * (inner - mean - normed * slope)


def gelu_terms(x):
    size = jnp.abs(x) * math.sqrt(0.5)
    t = 1.0 / (1.0 + 0.3275911 * size)
    bell = jnp.exp(-0.5 * x * x)
    poly = t * (0.254829592 + t * (-0.284496736 + t * (1.421413741 + t * (-1.453152027 + t * 1.061405429))))
    tail = 0.5 * poly * bell
    share = jnp.where(x >= 0.0, 1.0 - tail, tail)
    return x * share, share + x * bell * (1.0 / math.sqrt(2.0 * math.pi))


def block_kernel(
    numbers, x_ref, a_ref, out_ref, wide_ref, wide_b_ref, narrow_ref, branch_ref, gain_ref, shift_ref,
    block_ref, n1_ref, r1_ref, n2_ref, r2_ref, act_ref, slope_ref, sums_ref,
):
    shares = a_ref.shape[0]
    tile = x_ref.shape[0]
    x = x_ref[...].astype(f32)
    mixing = branch_ref[0:1, :]
    for s in range(shares):
        mixing = mixing + dot(a_ref[s, :, :96], out_ref[s, :96, :])
    middle, normed, rstd = norm_forward(x + mixing, gain_ref[0:1, :], shift_ref[0:1, :])
    n1_ref[...] = normed
    r1_ref[...] = rstd
    low = middle.astype(bf16)
    branch = branch_ref[1:2, :]
    width = wide_ref.shape[2]
    for s in range(shares):
        value, slope = gelu_terms(dot(low, wide_ref[s]) + wide_b_ref[s, 0:1, :])
        value = value.astype(bf16)
        act_ref[:, s * width : (s + 1) * width] = value
        slope_ref[:, s * width : (s + 1) * width] = slope.astype(bf16)
        branch = branch + dot(value, narrow_ref[s])
    block, normed, rstd = norm_forward(middle + branch, gain_ref[1:2, :], shift_ref[1:2, :])
    n2_ref[...] = normed
    r2_ref[...] = rstd
    block_ref[...] = block.astype(bf16)
    position = lax.broadcasted_iota(jnp.int32, (tile, 1), 0) + pl.program_id(0) * tile
    kept = jnp.where(position < numbers[0], 1.0, 0.0)
    row = lax.broadcasted_iota(jnp.int32, (8, x.shape[1]), 0)
    total = jnp.zeros((8, x.shape[1]), f32)
    for index, part in enumerate((x, mixing, branch)):
        total = jnp.where(row == index, jnp.sum(kept * part * part, axis=0, keepdims=True), total)

    @pl.when(pl.program_id(0) == 0)
    def _():
        sums_ref[...] = jnp.zeros_like(sums_ref)

    sums_ref[...] += total


def by_tile(tile, width):
    return pl.BlockSpec((tile, width), lambda i: (i, 0))


def block_forward(numbers, x, attended, w_out, w_wide, b_wide, w_narrow, branch_bias, gain, shift):
    rows, width = x.shape
    tile = min(TILE, rows)
    shares = attended.shape[0]
    units = shares * w_wide.shape[2]
    row, column = by_tile(tile, width), by_tile(tile, 1)
    return pl.pallas_call(
        block_kernel,
        grid=(rows // tile,),
        in_specs=[
            SMEM, row, pl.BlockSpec((shares, tile, 128), lambda i: (0, i, 0)), whole(w_out.shape),
            whole(w_wide.shape), whole(b_wide.shape), whole(w_narrow.shape), whole(branch_bias.shape),
            whole(gain.shape), whole(shift.shape),
        ],
        out_specs=[row, row, column, row, column, by_tile(tile, units), by_tile(tile, units), whole((8, width))],
        out_shape=[
            jax.ShapeDtypeStruct((rows, width), bf16),
            jax.ShapeDtypeStruct((rows, width), f32),
            jax.ShapeDtypeStruct((rows, 1), f32),
            jax.ShapeDtypeStruct((rows, width), f32),
            jax.ShapeDtypeStruct((rows, 1), f32),
            jax.ShapeDtypeStruct((rows, units), bf16),
            jax.ShapeDtypeStruct((rows, units), bf16),
            jax.ShapeDtypeStruct((8, width), f32),
        ],
        compiler_params=pltpu.CompilerParams(vmem_limit_bytes=VMEM),
        cost_estimate=cost(20),
        name="block_forward",
    )(numbers, x, attended, w_out, w_wide, b_wide, w_narrow, branch_bias, gain, shift)


def block_backward_kernel(
    d_ref, n1_ref, r1_ref, n2_ref, r2_ref, act_ref, slope_ref, a_ref, out_ref, wide_ref, narrow_ref, gain_ref,
    shift_ref, sum_ref, da_ref, g_ref, vec_ref, g_sum, low_s, branch_s, pre_s, mix_s,
):
    step = pl.program_id(0)
    shares = a_ref.shape[0]
    tile, width = d_ref.shape
    units = wide_ref.shape[2]
    span = pl.ds(pl.multiple_of(step * tile, tile), tile)

    @pl.when(step == 0)
    def _():
        vec_ref[...] = jnp.zeros_like(vec_ref)
        g_sum[...] = jnp.zeros_like(g_sum)

    def column(value):
        return jnp.sum(value, axis=0, keepdims=True)

    row = lax.broadcasted_iota(jnp.int32, (8, width), 0)
    d_block = d_ref[...]
    normed_two = n2_ref[...]
    d_two = norm_backward(d_block, normed_two, r2_ref[...], gain_ref[1:2, :])
    d_branch = d_two.astype(bf16)
    branch_s[span, :] = d_branch
    normed_one = n1_ref[...]
    low = (normed_one * gain_ref[0:1, :] + shift_ref[0:1, :]).astype(bf16)
    low_s[span, :] = low
    d_middle = d_two
    for s in range(shares):
        grad = dot(d_branch, narrow_ref[s], NT) * slope_ref[:, s * units : (s + 1) * units].astype(f32)
        grad = grad.astype(bf16)
        pre_s[span, s * units : (s + 1) * units] = grad
        g_sum[s : s + 1, :] += column(grad.astype(f32))
        d_middle = d_middle + dot(grad, wide_ref[s], NT)
    d_one = norm_backward(d_middle, normed_one, r1_ref[...], gain_ref[0:1, :])
    sum_ref[...] = d_one
    d_mixing = d_one.astype(bf16)
    mix_s[span, :] = d_mixing
    for s in range(shares):
        da_ref[s] = wide_rows(dot(d_mixing, out_ref[s, :96, :], NT)).astype(bf16)
    parts = (
        d_mixing.astype(f32), d_branch.astype(f32), d_middle * normed_one, d_block * normed_two, d_middle, d_block,
    )
    total = jnp.zeros((8, width), f32)
    for index, part in enumerate(parts):
        total = jnp.where(row == index, column(part), total)
    vec_ref[...] += total

    @pl.when(step == pl.num_programs(0) - 1)
    def _():
        for s in range(shares):
            part = slice(s * units, (s + 1) * units)
            g_ref[s, 0:units, :] = dot(act_ref[:, part], branch_s[...], TN).astype(bf16)
            g_ref[s, units : 2 * units, :] = dot(low_s[...], pre_s[:, part], TN).astype(bf16)
            g_ref[s, 2 * units : 2 * units + 96, :] = dot(a_ref[s], mix_s[...], TN)[:96].astype(bf16)
            first = lax.broadcasted_iota(jnp.int32, (32, units), 0) == 0
            g_ref[s, 2 * units + 96 : 2 * units + 128, :] = jnp.where(first, g_sum[s : s + 1, :], 0.0).astype(bf16)


def block_backward(d_block, n1, r1, n2, r2, act, slope, attended, w_out, w_wide, w_narrow, gain, shift):
    rows, width = d_block.shape
    tile = min(TILE, rows)
    shares, units = attended.shape[0], w_wide.shape[2]
    row, column = by_tile(tile, width), by_tile(tile, 1)
    return pl.pallas_call(
        block_backward_kernel,
        grid=(rows // tile,),
        in_specs=[
            row, row, column, row, column, whole(act.shape), by_tile(tile, shares * units), whole(attended.shape),
            whole(w_out.shape), whole(w_wide.shape), whole(w_narrow.shape), whole(gain.shape), whole(shift.shape),
        ],
        out_specs=[
            row,
            pl.BlockSpec((shares, tile, 128), lambda i: (0, i, 0)),
            whole((shares, 2 * units + 128, width)),
            whole((8, width)),
        ],
        out_shape=[
            jax.ShapeDtypeStruct((rows, width), f32),
            jax.ShapeDtypeStruct((shares, rows, 128), bf16),
            jax.ShapeDtypeStruct((shares, 2 * units + 128, width), bf16),
            jax.ShapeDtypeStruct((8, width), f32),
        ],
        scratch_shapes=[
            pltpu.VMEM((8, units), f32),
            pltpu.VMEM((rows, width), bf16),
            pltpu.VMEM((rows, width), bf16),
            pltpu.VMEM((rows, shares * units), bf16),
            pltpu.VMEM((rows, width), bf16),
        ],
        compiler_params=pltpu.CompilerParams(vmem_limit_bytes=VMEM),
        cost_estimate=cost(25),
        name="block_backward",
    )(d_block, n1, r1, n2, r2, act, slope, attended, w_out, w_wide, w_narrow, gain, shift)


def shift_shares(value, by):
    shares = lax.axis_size("heads")
    return lax.ppermute(value, "heads", [((i + by) % shares, i) for i in range(shares)])


def exchange(value, bit):
    size = lax.axis_size("batch")
    return lax.ppermute(value, "batch", [(i, i ^ bit) for i in range(size)])


def batch_sum(value):
    bit = 1
    while bit < lax.axis_size("batch"):
        low = value.astype(bf16) if value.dtype != f32 else value
        value = low.astype(f32) + exchange(low, bit).astype(f32)
        bit *= 2
        if low.dtype == bf16 and bit < lax.axis_size("batch"):
            value = value.astype(bf16)
    return value


def body(
    student_rows, teacher_rows, valid_length, split_point, project_five, bias_five, output_five, branch_bias,
    norm_gain, norm_bias, widen_weight, widen_bias, narrow_weight, project_six, bias_six, teacher_project,
    teacher_bias,
):
    shares = lax.axis_size("heads")
    batch = lax.axis_size("batch")
    me = lax.axis_index("heads")
    place = lax.axis_index("batch")
    all_rows = shares * batch * HEADS
    x = student_rows[0]
    teacher = teacher_rows[0]
    length = lax.dynamic_slice_in_dim(valid_length, me, 1)
    numbers = jnp.concatenate([length, lax.dynamic_slice_in_dim(split_point, me, 1)])

    def turned(weight):
        return jnp.transpose(weight, (1, 2, 0)).reshape(-1, weight.shape[0])

    def pad(rows, width):
        return jnp.pad(rows, ((0, 0), (0, width - rows.shape[1])))

    small = jnp.concatenate(
        [pad(bias_five, D), pad(bias_six, D), widen_bias[None], pad(teacher_bias, D), jnp.zeros((1, D), bf16)], axis=0
    )
    five = turned(project_five)
    fives = [five] + [shift_shares(five, by) for by in range(1, shares)]
    smalls = [small] + [shift_shares(small, by) for by in range(1, shares)]
    smalls = [s.astype(f32) for s in smalls]

    def eighth(rows):
        count = -(-rows.shape[0] // batch)
        rows = jnp.pad(rows, ((0, count * batch - rows.shape[0]), (0, 0)))
        return lax.dynamic_slice_in_dim(rows, place * count, count)

    def gather(rows):
        part = eighth(rows)
        parts = [shift_shares(part, by) for by in range(1, shares)]
        return [rows] + [lax.all_gather(p, "batch", axis=0, tiled=True)[: rows.shape[0]] for p in parts]

    units = widen_weight.shape[1]
    mid = jnp.concatenate([widen_weight, narrow_weight, jnp.pad(output_five, ((0, 32), (0, 0)))], axis=0)
    mids = gather(mid)
    sixes = gather(turned(project_six))
    taughts = gather(turned(teacher_project))

    heads = []
    for s in range(shares):
        heads.append(attend_forward(length, x, fives[s], smalls[s][0:2]))
    attended = jnp.stack([h[5] for h in heads])
    mids = jnp.stack(mids)
    smalls = jnp.stack(smalls)
    w_wide, w_narrow, w_out = mids[:, :D], mids[:, D : D + units], mids[:, D + units :]
    block, n1, r1, n2, r2, act, slope, squares = block_forward(
        numbers, x, attended, w_out, w_wide, smalls[:, 4:5], w_narrow, branch_bias, norm_gain, norm_bias
    )
    d_block, g_six, divergence = relations(
        numbers, block, teacher, jnp.stack(sixes), smalls[:, 2:4], jnp.stack(taughts), smalls[:, 5:7], all_rows
    )
    d_sum_one, d_attended, g_mid, vectors = block_backward(
        d_block, n1, r1, n2, r2, act, slope, attended, w_out, w_wide, w_narrow, norm_gain, norm_bias
    )

    def to_owner(parts):
        total = parts[0].astype(f32)
        for by in range(1, shares):
            total = total + shift_shares(parts[by], shares - by).astype(f32)
        return total.astype(bf16)

    six = batch_sum(to_owner([g_six[s] for s in range(shares)]))

    counts = g_mid.shape[1] // batch
    mid_part = lax.psum_scatter(g_mid, "batch", scatter_dimension=1, tiled=True)
    mid_part = to_owner([mid_part[s] for s in range(shares)])
    mid_sum = lax.all_gather(mid_part, "batch", axis=0, tiled=True).astype(f32)

    kept = jnp.sum(jnp.where(jnp.arange(x.shape[0]) < length, 1.0, 0.0))
    scalars = jnp.stack([jnp.sum(divergence), jnp.sum(squares[0]), jnp.sum(squares[1]), jnp.sum(squares[2]), kept])
    vectors = lax.dynamic_update_slice(vectors, pad(scalars[None], D), (6, 0))
    bit = 1
    while bit < shares:
        vectors = vectors + lax.ppermute(vectors, "heads", [(i, i ^ bit) for i in range(shares)])
        bit *= 2
    vectors = batch_sum(vectors)

    grad_in = d_sum_one
    g_five = [None] * shares
    for s in list(range(1, shares)) + [0]:
        q, k, v, e, r, a = heads[s]
        g_five[s], grad_in = attend_backward(q, k, v, e, r, a, d_attended[s], x, fives[s], grad_in)
    five_sum = batch_sum(to_owner(g_five))

    def unturned(grad):
        return jnp.transpose(grad[: 3 * 96].reshape(3, 96, -1), (2, 0, 1))

    totals = vectors[6]
    counted = totals[4] * D
    summary = jnp.concatenate([totals[:1], jnp.sqrt(totals[1:4] / counted)])
    return (
        block[None], grad_in[None], unturned(five_sum), five_sum[288:290, :96],
        mid_sum[2 * units : 2 * units + 96], vectors[0:2], vectors[2:4], vectors[4:6],
        mid_sum[units : 2 * units], mid_sum[2 * units + 96], mid_sum[:units],
        unturned(six), six[288:290, :96], summary,
    )


def solution(mesh):
    return jax.shard_map(
        body,
        mesh=mesh,
        in_specs=(
            P(("batch", "heads"), None, None),
            P(("batch", "heads"), None, None),
            P("batch"),
            P("batch"),
            P(None, None, "heads"),
            P(None, "heads"),
            P("heads", None),
            P(),
            P(),
            P(),
            P(None, "heads"),
            P("heads"),
            P("heads", None),
            P(None, None, "heads"),
            P(None, "heads"),
            P(None, None, "heads"),
            P(None, "heads"),
        ),
        out_specs=(
            P(("batch", "heads"), None, None),
            P(("batch", "heads"), None, None),
            P(None, None, "heads"),
            P(None, "heads"),
            P("heads", None),
            P(),
            P(),
            P(),
            P(None, "heads"),
            P("heads"),
            P("heads", None),
            P(None, None, "heads"),
            P(None, "heads"),
            P(),
        ),
        check_vma=False,
    )
```

time: 985 us -> 535 us (0.54)
  waiting for transfers between devices: 308 us -> 30.7 us
  local copies, waits for them, and re-layouts: 139 us -> 18.8 us
  blocking collectives: 180 us -> 96.7 us
  Pallas kernels: 220 us -> 299 us
  matrix products: 74.7 us -> 0 us
  starting transfers between devices: 0.28 us -> 44.2 us
  other arithmetic: 33.7 us -> 21.6 us
    unnamed x11 -> x1, waiting for transfers between devices: 308 us -> 0.02 us
    unnamed x103 -> x24, local copies, waits for them, and re-layouts: 97.4 us -> 0.06 us
    pallas_call x3 -> x11, Pallas kernels: 220 us -> 299 us  [the longest x1 167 us: relations(): pl.pallas_call(functools.partial(relation_kernel, all_rows=all_rows), gri...]
    dot_general x16 -> x0, matrix products: 74.7 us -> none  [dot(): return lax.dot_general(left, right, dims, preferred_element_type=f32)]
    ppermute x0 -> x35, starting transfers between devices: none -> 44.1 us  [the longest x24 31.4 us: shift_shares(): lax.ppermute(value, 'heads', [((i + by) % shares, i) for i in range(share...]
    all_gather x10, blocking collectives: 139 us -> 96.7 us  [the longest x9 87.1 us: gather(): lax.all_gather(p, 'batch', axis=0, tiled=True)[:rows.shape[0]]]
    psum x1 -> x0, blocking collectives: 40.3 us -> none  [body(): lax.psum(jnp.concatenate([p.reshape(-1) for p in vectors]), ('heads', 'ba...]
    ppermute x0 -> x35, waiting for transfers between devices: none -> 30.7 us  [the longest x24 17.8 us: shift_shares(): lax.ppermute(value, 'heads', [((i + by) % shares, i) for i in range(share...]
  transfers between devices with their start and end apart: 7 -> 36, of which waited for: 4 -> 7; matrix products, arithmetic and copies ran while one was open for 17% -> 5% of each run, Pallas kernels for 4% -> 16%
where the time goes in v2:
time: 535 us; the launch traced here: 526 us
  Pallas kernels  299 us (56%)
  blocking collectives  96.7 us (18%)
  starting transfers between devices  44.2 us (8%)
  waiting for transfers between devices  30.7 us (6%)
  other arithmetic  21.6 us (4%)
  local copies, waits for them, and re-layouts  18.8 us (4%)
  between operations  15.4 us (3%)
    pallas_call x1, Pallas kernels, relations(): pl.pallas_call(functools.partial(relation_kernel, all_rows=all_rows), gri...  167 us
    all_gather x9, blocking collectives, gather(): lax.all_gather(p, 'batch', axis=0, tiled=True)[:rows.shape[0]]  87.1 us
    pallas_call x4, Pallas kernels, attend_backward(): pl.pallas_call(attend_backward_kernel, grid=(1,), in_specs=[row, row, row...  55 us
    pallas_call x4, Pallas kernels, attend_forward(): pl.pallas_call(attend_forward_kernel, grid=(1,), in_specs=[SMEM, whole(x....  40.7 us
    ppermute x24, starting transfers between devices, shift_shares(): lax.ppermute(value, 'heads', [((i + by) % shares, i) for i in range(share...  31.4 us
    pallas_call x1, Pallas kernels, block_backward(): pl.pallas_call(block_backward_kernel, grid=(rows // tile,), in_specs=[row...  18.9 us
    ppermute x24, waiting for transfers between devices, shift_shares(): lax.ppermute(value, 'heads', [((i + by) % shares, i) for i in range(share...  17.8 us
    pallas_call x1, Pallas kernels, block_forward(): pl.pallas_call(block_kernel, grid=(rows // tile,), in_specs=[SMEM, row, p...  16.7 us
  transfers between devices with their start and end apart: 36, of which 7 were waited for; matrix products, arithmetic and copies ran while one was open for 5% of the time, Pallas kernels for 16%

profile of v2, /device:TPU:0, one launch (start us, length us, event | category | flops | bytes accessed | tf_op | source)
XLA Modules:
  0.0 526.0 jit_solution(15279766802258411245)
XLA Ops:
  8.7 1.3 pad_bitcast_fusion
  10.0 5.1 collective-permute-start.1
  15.5 2.5 collective-permute-start.2
  18.0 2.0 collective-permute-start.5
  20.0 1.2 dynamic_slice.15.length_ref
  21.3 1.2 dynamic_slice.16
  22.5 1.2 fusion.10
  23.9 10.2 %attend_forward.4 = (bf16[1024,128]{1,0:T(8,128)(2,1)}, bf16[1024,128]{1,0:T(8,128)(2,1)}, bf16[1024,128]{1,0:T(8,128)(2,1)}, bf16[3,1024,1024]{2,1,0:T(8,128)(2...) custom-call(s32[1]{0:T(128)} %dynamic_slice.15.length_ref, bf16[1024,384]{1,0:T(8,128)(2,1)} %bitcast.113, ...), custom_call_target="tpu_custom_call" | custom-call | flops 9900000256 | bytes 1024 | tf_op jit(solution)/shard_map/attend_forward/pallas_call | solution.py:211
  34.0 1.9 pad_add_fusion.numbers
  36.0 1.2 select_reduce_fusion
  37.2 2.3 collective-permute-start.10
  39.6 2.0 collective-permute-start.11
  44.6 2.0 collective-permute-done.10
  46.6 9.3 %all-gather.1 = bf16[8,36,384]{2,1,0:T(8,128)(2,1)S(1)} all-gather(bf16[1,36,384]{2,1,0:T(8,128)(2,1)S(1)} %bitcast.109), channel_id=1, replica_groups=mesh['heads'=4,'batch'=8] {'batch'}, dimensions={0}, use_global_device_ids=true | all-gather | bytes 248832 | tf_op jit(solution)/shard_map/all_gather | solution.py:899
  56.0 1.6 collective-permute-start.7
  57.6 9.3 %all-gather.2 = bf16[8,36,384]{2,1,0:T(8,128)(2,1)S(1)} all-gather(bf16[1,36,384]{2,1,0:T(8,128)(2,1)S(1)} %bitcast.108), channel_id=1, replica_groups=mesh['heads'=4,'batch'=8] {'batch'}, dimensions={0}, use_global_device_ids=true | all-gather | bytes 248832 | tf_op jit(solution)/shard_map/all_gather | solution.py:899
  67.5 8.3 %all-gather = bf16[8,36,384]{2,1,0:T(8,128)(2,1)S(1)} all-gather(bf16[1,36,384]{2,1,0:T(8,128)(2,1)S(1)} %bitcast.110), channel_id=1, replica_groups=mesh['heads'=4,'batch'=8] {'batch'}, dimensions={0}, use_global_device_ids=true | all-gather | bytes 248832 | tf_op jit(solution)/shard_map/all_gather | solution.py:899
  75.9 1.1 pad_maximum_fusion.6.w_ref
  76.9 3.3 collective-permute-start.6
  80.3 10.2 %all_gather.31 = bf16[896,384]{1,0:T(8,128)(2,1)S(1)} all-gather(bf16[112,384]{1,0:T(8,128)(2,1)S(1)} %collective-permute-done.7), channel_id=1, replica_groups=mesh['heads'=4,'batch'=8] {'batch'}, dimensions={0}, use_global_device_ids=true | all-gather | bytes 774144 | tf_op jit(solution)/shard_map/all_gather | solution.py:899
  90.5 1.1 collective-permute-start.12
  91.6 9.3 %all_gather.32 = bf16[896,384]{1,0:T(8,128)(2,1)S(1)} all-gather(bf16[112,384]{1,0:T(8,128)(2,1)S(1)} %collective-permute-done.8), channel_id=1, replica_groups=mesh['heads'=4,'batch'=8] {'batch'}, dimensions={0}, use_global_device_ids=true | all-gather | bytes 774144 | tf_op jit(solution)/shard_map/all_gather | solution.py:899
  100.8 10.2 %all_gather.30 = bf16[896,384]{1,0:T(8,128)(2,1)S(1)} all-gather(bf16[112,384]{1,0:T(8,128)(2,1)S(1)} %collective-permute-done.6), channel_id=1, replica_groups=mesh['heads'=4,'batch'=8] {'batch'}, dimensions={0}, use_global_device_ids=true | all-gather | bytes 774144 | tf_op jit(solution)/shard_map/all_gather | solution.py:899
  111.1 1.7 pad_maximum_fusion.1
  112.7 0.8 pad_maximum_fusion.7.out_ref
  113.5 1.0 collective-permute-start.14
  114.5 9.7 %all_gather.36 = bf16[576,768]{1,0:T(8,128)(2,1)S(1)} all-gather(bf16[72,768]{1,0:T(8,128)(2,1)S(1)} %collective-permute-done.12), channel_id=1, replica_groups=mesh['heads'=4,'batch'=8] {'batch'}, dimensions={0}, use_global_device_ids=true | all-gather | bytes 995328 | tf_op jit(solution)/shard_map/all_gather | solution.py:899
  124.2 10.7 %all_gather.37 = bf16[576,768]{1,0:T(8,128)(2,1)S(1)} all-gather(bf16[72,768]{1,0:T(8,128)(2,1)S(1)} %collective-permute-done.13), channel_id=1, replica_groups=mesh['heads'=4,'batch'=8] {'batch'}, dimensions={0}, use_global_device_ids=true | all-gather | bytes 995328 | tf_op jit(solution)/shard_map/all_gather | solution.py:899
  134.9 10.1 %all_gather.38 = bf16[576,768]{1,0:T(8,128)(2,1)S(1)} all-gather(bf16[72,768]{1,0:T(8,128)(2,1)S(1)} %collective-permute-done.14), channel_id=1, replica_groups=mesh['heads'=4,'batch'=8] {'batch'}, dimensions={0}, use_global_device_ids=true | all-gather | bytes 995328 | tf_op jit(solution)/shard_map/all_gather | solution.py:899
  145.0 2.0 pad_maximum_fusion.tw_ref
  147.1 10.2 %attend_forward.5 = (bf16[1024,128]{1,0:T(8,128)(2,1)}, bf16[1024,128]{1,0:T(8,128)(2,1)}, bf16[1024,128]{1,0:T(8,128)(2,1)}, bf16[3,1024,1024]{2,1,0:T(8,128)(2...) custom-call(s32[1]{0:T(128)} %dynamic_slice.15.length_ref, bf16[1024,384]{1,0:T(8,128)(2,1)} %bitcast.114, ...), custom_call_target="tpu_custom_call" | custom-call | flops 9900000256 | bytes 1024 | tf_op jit(solution)/shard_map/attend_forward/pallas_call | solution.py:211
  157.3 10.1 %attend_forward.6 = (bf16[1024,128]{1,0:T(8,128)(2,1)}, bf16[1024,128]{1,0:T(8,128)(2,1)}, bf16[1024,128]{1,0:T(8,128)(2,1)}, bf16[3,1024,1024]{2,1,0:T(8,128)(2...) custom-call(s32[1]{0:T(128)} %dynamic_slice.15.length_ref, bf16[1024,384]{1,0:T(8,128)(2,1)} %bitcast.115, ...), custom_call_target="tpu_custom_call" | custom-call | flops 9900000256 | bytes 1024 | tf_op jit(solution)/shard_map/attend_forward/pallas_call | solution.py:211
  167.5 10.2 %attend_forward.7 = (bf16[1024,128]{1,0:T(8,128)(2,1)}, bf16[1024,128]{1,0:T(8,128)(2,1)}, bf16[1024,128]{1,0:T(8,128)(2,1)}, bf16[3,1024,1024]{2,1,0:T(8,128)(2...) custom-call(s32[1]{0:T(128)} %dynamic_slice.15.length_ref, bf16[1024,384]{1,0:T(8,128)(2,1)} %bitcast.116, ...), custom_call_target="tpu_custom_call" | custom-call | flops 9900000256 | bytes 1024 | tf_op jit(solution)/shard_map/attend_forward/pallas_call | solution.py:211
  177.7 2.1 pad_maximum_fusion.5.a_ref
  179.8 16.7 %block_forward.1 = (bf16[1024,384]{1,0:T(8,128)(2,1)}, f32[1024,384]{1,0:T(8,128)}, f32[1024,1]{1,0:T(8,128)}, f32[1024,384]{1,0:T(8,128)}, f32[1024,1]{1,0:T(8,...) custom-call(s32[2]{0:T(128)} %pad_add_fusion.numbers, ...), custom_call_target="tpu_custom_call" | custom-call | flops 22000001024 | bytes 1024 | tf_op jit(solution)/shard_map/block_forward/pallas_call | solution.py:720
  196.6 1.4 slice_reduce_fusion.1
  198.0 167.2 %relations.1 = (f32[1024,384]{1,0:T(8,128)}, bf16[4,304,384]{2,1,0:T(8,128)(2,1)}, f32[1024,1]{1,0:T(8,128)}) custom-call(s32[2]{0:T(128)} %pad_add_fusion.numbers, bf16[1024,384]{1,0:T(8,128)(2,1)} %get-tuple-element.65.block_ref, bf16[1024,768]{1,0:T(8,128)(2,1)} %bitcast.112, bf16[4,288,384]{2,1,0:T(8,128)(2,1)} %pad_maximum_fusion.6.w_ref, ...), custom_call_target="tpu_custom_call" | custom-call | flops 121000001536 | bytes 1024 | tf_op jit(solution)/shard_map/relations/pallas_call | solution.py:609
  365.2 1.8 reduce_sum.45
  367.0 3.2 stack.112
  370.2 18.9 %block_backward.1 = (f32[1024,384]{1,0:T(8,128)}, bf16[4,1024,128]{2,1,0:T(8,128)(2,1)}, bf16[4,896,384]{2,1,0:T(8,128)(2,1)}, f32[8,384]{1,0:T(8,128)}) custom-call(f32[1024,384]{1,0:T(8,128)} %get-tuple-element.71.d_ref, f32[1024,384]{1,0:T(8,128)} %get-tuple-element.72.n1_ref, f32[1024,1]{1,0:T(8,128)} %get-tuple-element.73.r1_ref, ...), custom_call_target="tpu_custom_call" | custom-call | flops 27499999232 | bytes 1024 | tf_op jit(solution)/shard_map/block_backward/pallas_call | solution.py:809
  389.2 1.3 dynamic_update_slice.3
  390.6 2.1 collective-permute-start.29
  392.7 2.4 collective-permute-start.31
  395.2 1.0 slice_bitcast_fusion
  396.1 1.5 collective-permute-start.25
  397.6 13.7 %attend_backward.4 = (bf16[304,384]{1,0:T(8,128)(2,1)}, f32[1024,384]{1,0:T(8,128)}) custom-call(bf16[1024,128]{1,0:T(8,128)(2,1)} %get-tuple-element.89.q_ref, bf16[1024,128]{1,0:T(8,128)(2,1)} %get-tuple-element.90.k_ref, bf16[1024,128]{1,0:T(8,128)(2,1)} %get-tuple-element.91.v_ref, bf16[3,1024,1024]{2,1,0:T(8,128)(2,1)} %get-tuple-element.92.e_hbm, ...), custom_call_target="tpu_custom_call" | custom-call | flops 11000000512 | bytes 1024 | tf_op jit(solution)/shard_map/attend_backward/pallas_call | solution.py:341
  411.4 13.7 %attend_backward.5 = (bf16[304,384]{1,0:T(8,128)(2,1)}, f32[1024,384]{1,0:T(8,128)}) custom-call(bf16[1024,128]{1,0:T(8,128)(2,1)} %get-tuple-element.84.q_ref, bf16[1024,128]{1,0:T(8,128)(2,1)} %get-tuple-element.85.k_ref, bf16[1024,128]{1,0:T(8,128)(2,1)} %get-tuple-element.86.v_ref, bf16[3,1024,1024]{2,1,0:T(8,128)(2,1)} %get-tuple-element.87.e_hbm, ...), custom_call_target="tpu_custom_call" | custom-call | flops 11000000512 | bytes 1024 | tf_op jit(solution)/shard_map/attend_backward/pallas_call | solution.py:341
  425.1 6.9 %collective-permute-start.27 = (f32[8,384]{1,0:T(8,128)S(1)}, f32[8,384]{1,0:T(8,128)S(1)}, u32[]{:S(2)}, u32[]{:S(2)}) collective-permute-start(f32[8,384]{1,0:T(8,128)S(1)} %add.100), channel_id=1, source_target_pairs={{0,2},{1,3},{2,0},{3,1},{4,6},{5,7},{6,4},{7,5},{8,10},{9,11},{10,... | collective-permute-start | bytes 36872 | tf_op jit(solution)/shard_map/ppermute | solution.py:848
  432.0 13.9 %attend_backward.6 = (bf16[304,384]{1,0:T(8,128)(2,1)}, f32[1024,384]{1,0:T(8,128)}) custom-call(bf16[1024,128]{1,0:T(8,128)(2,1)} %get-tuple-element.79.q_ref, bf16[1024,128]{1,0:T(8,128)(2,1)} %get-tuple-element.80.k_ref, bf16[1024,128]{1,0:T(8,128)(2,1)} %get-tuple-element.81.v_ref, bf16[3,1024,1024]{2,1,0:T(8,128)(2,1)} %get-tuple-element.82.e_hbm, ...), custom_call_target="tpu_custom_call" | custom-call | flops 11000000512 | bytes 1024 | tf_op jit(solution)/shard_map/attend_backward/pallas_call | solution.py:341
  446.3 1.6 collective-permute-start.28
  447.9 13.7 %attend_backward.7 = (bf16[304,384]{1,0:T(8,128)(2,1)}, f32[1024,384]{1,0:T(8,128)}) custom-call(bf16[1024,128]{1,0:T(8,128)(2,1)} %get-tuple-element.66.q_ref, bf16[1024,128]{1,0:T(8,128)(2,1)} %get-tuple-element.67.k_ref, bf16[1024,128]{1,0:T(8,128)(2,1)} %get-tuple-element.68.v_ref, bf16[3,1024,1024]{2,1,0:T(8,128)(2,1)} %get-tuple-element.69.e_hbm, ...), custom_call_target="tpu_custom_call" | custom-call | flops 11000000512 | bytes 1024 | tf_op jit(solution)/shard_map/attend_backward/pallas_call | solution.py:341
  463.0 1.2 pad_maximum_fusion.13
  465.7 14.0 %collective-permute-done.16 = bf16[304,384]{1,0:T(8,128)(2,1)S(1)} collective-permute-done((bf16[304,384]{1,0:T(8,128)(2,1)S(1)}, bf16[304,384]{1,0:T(8,128)(2,1)S(1)}, u32[]{:S(2)}, u32[]{:S(2)}) %collective-permute-start.16) | collective-permute-done | bytes 233504 | tf_op jit(solution)/shard_map/ppermute | solution.py:843
  479.7 1.1 add_convert_fusion.4
  481.4 1.0 collective-permute-done.18
  483.2 6.3 %collective-permute-done.33 = bf16[304,384]{1,0:T(8,128)(2,1)S(1)} collective-permute-done((bf16[304,384]{1,0:T(8,128)(2,1)S(1)}, bf16[304,384]{1,0:T(8,128)(2,1)S(1)}, u32[]{:S(2)}, u32[]{:S(2)}) %collective-permute-start.33) | collective-permute-done | bytes 233504 | tf_op jit(solution)/shard_map/ppermute | solution.py:848
  490.3 3.8 collective-permute-done.19
  494.9 1.7 collective-permute-done.34
  496.6 1.0 slice_bitcast_fusion.9
  498.0 3.5 collective-permute-start.23
  504.3 1.7 collective-permute-done.22
  506.1 0.9 fusion.7
  507.0 9.5 %all_gather.39 = bf16[896,384]{1,0:T(8,128)(2,1)S(1)} all-gather(bf16[112,384]{1,0:T(8,128)(2,1)S(1)} %fusion.7), channel_id=1, replica_groups=mesh['heads'=4,'batch'=8] {'batch'}, dimensions={0}, use_global_device_ids=true | all-gather | bytes 774144 | tf_op jit(solution)/shard_map/all_gather | solution.py:935
  516.6 1.1 fusion.11
  (121 shorter events, 16.1 us)
Async XLA Ops:
  7.2 16.6 %copy-start = (bf16[768,3,192]{0,2,1:T(8,128)(2,1)S(1)}, bf16[768,3,192]{0,2,1:T(8,128)(2,1)}, u32[]{:S(2)}) copy-start(bf16[768,3,192]{0,2,1:T(8,128)(2,1)} %param.32) | copy-start | bytes 2654212
  7.2 16.6 %copy-start.3 = (bf16[384,3,96]{0,2,1:T(8,128)(2,1)S(1)}, bf16[384,3,96]{0,2,1:T(8,128)(2,1)}, u32[]{:S(2)}) copy-start(bf16[384,3,96]{0,2,1:T(8,128)(2,1)} %param.30) | copy-start | bytes 663556
  7.2 489.4 %reduce-scatter.2.cloned.1.call-start = ((), (), s32[]{:S(2)}) async-start(), calls=%async_computation.1 | async-start | bytes 3096576 | tf_op jit(solution)/shard_map/reduce_scatter | solution.py:933
  10.0 29.6 %collective-permute-start.1 = (bf16[8,384]{1,0:T(8,128)(2,1)S(1)}, bf16[8,384]{1,0:T(8,128)(2,1)S(1)}, u32[]{:S(2)}, u32[]{:S(2)}) collective-permute-start(bf16[8,384]{1,0:T(8,128)(2,1)S(1)} %concatenate.30), channel_id=1, source_target_pairs={{8,0},{16,8},{24,16},{0,24},{9,1},{17,9},{25,17},{1,25},{10,2},{18... | collective-permute-start | bytes 18440 | tf_op jit(solution)/shard_map/ppermute | solution.py:843
  15.1 22.2 %collective-permute-start.3 = (bf16[8,384]{1,0:T(8,128)(2,1)S(1)}, bf16[8,384]{1,0:T(8,128)(2,1)S(1)}, u32[]{:S(2)}, u32[]{:S(2)}) collective-permute-start(bf16[8,384]{1,0:T(8,128)(2,1)S(1)} %concatenate.30), channel_id=1, source_target_pairs={{16,0},{24,8},{0,16},{8,24},{17,1},{25,9},{1,17},{9,25},{18,2},{26... | collective-permute-start | bytes 18440 | tf_op jit(solution)/shard_map/ppermute | solution.py:843
  15.1 132.0 %collective-permute-start = (bf16[288,384]{1,0:T(8,128)(2,1)}, bf16[288,384]{1,0:T(8,128)(2,1)}, u32[]{:S(2)}, u32[]{:S(2)}) collective-permute-start(bf16[288,384]{1,0:T(8,128)(2,1)} %bitcast.122), channel_id=1, source_target_pairs={{8,0},{16,8},{24,16},{0,24},{9,1},{17,9},{25,17},{1,25},{10,2},{18... | collective-permute-start | bytes 663560 | tf_op jit(solution)/shard_map/ppermute | solution.py:843
  15.5 141.7 %collective-permute-start.2 = (bf16[288,384]{1,0:T(8,128)(2,1)}, bf16[288,384]{1,0:T(8,128)(2,1)}, u32[]{:S(2)}, u32[]{:S(2)}) collective-permute-start(bf16[288,384]{1,0:T(8,128)(2,1)} %bitcast.123), channel_id=1, source_target_pairs={{16,0},{24,8},{0,16},{8,24},{17,1},{25,9},{1,17},{9,25},{18,2},{26... | collective-permute-start | bytes 663560 | tf_op jit(solution)/shard_map/ppermute | solution.py:843
  18.0 19.2 %collective-permute-start.5 = (bf16[8,384]{1,0:T(8,128)(2,1)S(1)}, bf16[8,384]{1,0:T(8,128)(2,1)S(1)}, u32[]{:S(2)}, u32[]{:S(2)}) collective-permute-start(bf16[8,384]{1,0:T(8,128)(2,1)S(1)} %concatenate.30), channel_id=1, source_target_pairs={{24,0},{0,8},{8,16},{16,24},{25,1},{1,9},{9,17},{17,25},{26,2},{2,... | collective-permute-start | bytes 18440 | tf_op jit(solution)/shard_map/ppermute | solution.py:843
  23.8 12.1 %copy-start.8 = (bf16[384]{0:T(512)(128)(2,1)S(1)}, bf16[384]{0:T(512)(128)(2,1)}, u32[]{:S(2)}) copy-start(bf16[384]{0:T(512)(128)(2,1)} %param.28) | copy-start | bytes 2308
  23.8 13.4 %copy-start.11 = (bf16[384,3,96]{0,2,1:T(8,128)(2,1)S(1)}, bf16[384,3,96]{0,2,1:T(8,128)(2,1)}, u32[]{:S(2)}) copy-start(bf16[384,3,96]{0,2,1:T(8,128)(2,1)} %param.21) | copy-start | bytes 663556
  37.2 130.2 %collective-permute-start.4 = (bf16[288,384]{1,0:T(8,128)(2,1)S(1)}, bf16[288,384]{1,0:T(8,128)(2,1)}, u32[]{:S(2)}, u32[]{:S(2)}) collective-permute-start(bf16[288,384]{1,0:T(8,128)(2,1)S(1)} %bitcast.126), channel_id=1, source_target_pairs={{24,0},{0,8},{8,16},{16,24},{25,1},{1,9},{9,17},{17,25},{26,2},{2,... | collective-permute-start | bytes 663560 | tf_op jit(solution)/shard_map/ppermute | solution.py:843
  37.2 9.4 %collective-permute-start.10 = (bf16[36,384]{1,0:T(8,128)(2,1)S(1)}, bf16[36,384]{1,0:T(8,128)(2,1)S(1)}, u32[]{:S(2)}, u32[]{:S(2)}) collective-permute-start(bf16[36,384]{1,0:T(8,128)(2,1)S(1)} %constant_dynamic-slice_fusion.1), channel_id=1, source_target_pairs={{16,0},{24,8},{0,16},{8,24},{17,1},{25,9},{1,17},{9,25},{18,2},{26... | collective-permute-start | bytes 82952 | tf_op jit(solution)/shard_map/ppermute | solution.py:843
  39.6 16.4 %collective-permute-start.11 = (bf16[36,384]{1,0:T(8,128)(2,1)S(1)}, bf16[36,384]{1,0:T(8,128)(2,1)S(1)}, u32[]{:S(2)}, u32[]{:S(2)}) collective-permute-start(bf16[36,384]{1,0:T(8,128)(2,1)S(1)} %constant_dynamic-slice_fusion.1), channel_id=1, source_target_pairs={{24,0},{0,8},{8,16},{16,24},{25,1},{1,9},{9,17},{17,25},{26,2},{2,... | collective-permute-start | bytes 82952 | tf_op jit(solution)/shard_map/ppermute | solution.py:843
  46.6 20.3 %collective-permute-start.9 = (bf16[36,384]{1,0:T(8,128)(2,1)S(1)}, bf16[36,384]{1,0:T(8,128)(2,1)S(1)}, u32[]{:S(2)}, u32[]{:S(2)}) collective-permute-start(bf16[36,384]{1,0:T(8,128)(2,1)S(1)} %constant_dynamic-slice_fusion.1), channel_id=1, source_target_pairs={{8,0},{16,8},{24,16},{0,24},{9,1},{17,9},{25,17},{1,25},{10,2},{18... | collective-permute-start | bytes 82952 | tf_op jit(solution)/shard_map/ppermute | solution.py:843
  56.0 21.0 %collective-permute-start.7 = (bf16[112,384]{1,0:T(8,128)(2,1)S(1)}, bf16[112,384]{1,0:T(8,128)(2,1)S(1)}, u32[]{:S(2)}, u32[]{:S(2)}) collective-permute-start(bf16[112,384]{1,0:T(8,128)(2,1)S(1)} %constant_dynamic-slice_fusion.2), channel_id=1, source_target_pairs={{16,0},{24,8},{0,16},{8,24},{17,1},{25,9},{1,17},{9,25},{18,2},{26... | collective-permute-start | bytes 258056 | tf_op jit(solution)/shard_map/ppermute | solution.py:843
  66.9 23.6 %collective-permute-start.8 = (bf16[112,384]{1,0:T(8,128)(2,1)S(1)}, bf16[112,384]{1,0:T(8,128)(2,1)S(1)}, u32[]{:S(2)}, u32[]{:S(2)}) collective-permute-start(bf16[112,384]{1,0:T(8,128)(2,1)S(1)} %constant_dynamic-slice_fusion.2), channel_id=1, source_target_pairs={{24,0},{0,8},{8,16},{16,24},{25,1},{1,9},{9,17},{17,25},{26,2},{2,... | collective-permute-start | bytes 258056 | tf_op jit(solution)/shard_map/ppermute | solution.py:843
  76.9 23.9 %collective-permute-start.6 = (bf16[112,384]{1,0:T(8,128)(2,1)S(1)}, bf16[112,384]{1,0:T(8,128)(2,1)S(1)}, u32[]{:S(2)}, u32[]{:S(2)}) collective-permute-start(bf16[112,384]{1,0:T(8,128)(2,1)S(1)} %constant_dynamic-slice_fusion.2), channel_id=1, source_target_pairs={{8,0},{16,8},{24,16},{0,24},{9,1},{17,9},{25,17},{1,25},{10,2},{18... | collective-permute-start | bytes 258056 | tf_op jit(solution)/shard_map/ppermute | solution.py:843
  90.5 23.1 %collective-permute-start.12 = (bf16[72,768]{1,0:T(8,128)(2,1)S(1)}, bf16[72,768]{1,0:T(8,128)(2,1)S(1)}, u32[]{:S(2)}, u32[]{:S(2)}) collective-permute-start(bf16[72,768]{1,0:T(8,128)(2,1)S(1)} %constant_dynamic-slice_fusion), channel_id=1, source_target_pairs={{8,0},{16,8},{24,16},{0,24},{9,1},{17,9},{25,17},{1,25},{10,2},{18... | collective-permute-start | bytes 331784 | tf_op jit(solution)/shard_map/ppermute | solution.py:843
  100.8 23.4 %collective-permute-start.13 = (bf16[72,768]{1,0:T(8,128)(2,1)S(1)}, bf16[72,768]{1,0:T(8,128)(2,1)S(1)}, u32[]{:S(2)}, u32[]{:S(2)}) collective-permute-start(bf16[72,768]{1,0:T(8,128)(2,1)S(1)} %constant_dynamic-slice_fusion), channel_id=1, source_target_pairs={{16,0},{24,8},{0,16},{8,24},{17,1},{25,9},{1,17},{9,25},{18,2},{26... | collective-permute-start | bytes 331784 | tf_op jit(solution)/shard_map/ppermute | solution.py:843
  113.5 21.4 %collective-permute-start.14 = (bf16[72,768]{1,0:T(8,128)(2,1)S(1)}, bf16[72,768]{1,0:T(8,128)(2,1)S(1)}, u32[]{:S(2)}, u32[]{:S(2)}) collective-permute-start(bf16[72,768]{1,0:T(8,128)(2,1)S(1)} %constant_dynamic-slice_fusion), channel_id=1, source_target_pairs={{24,0},{0,8},{8,16},{16,24},{25,1},{1,9},{9,17},{17,25},{26,2},{2,... | collective-permute-start | bytes 331784 | tf_op jit(solution)/shard_map/ppermute | solution.py:843
  167.4 10.3 %copy-start.4 = (bf16[1024,128]{1,0:T(8,128)(2,1)S(1)}, bf16[1024,128]{1,0:T(8,128)(2,1)}, u32[]{:S(2)}) copy-start(bf16[1024,128]{1,0:T(8,128)(2,1)} %get-tuple-element.61.a_ref) | copy-start | bytes 786436
  167.4 10.3 %copy-start.5 = (bf16[1024,128]{1,0:T(8,128)(2,1)S(1)}, bf16[1024,128]{1,0:T(8,128)(2,1)}, u32[]{:S(2)}) copy-start(bf16[1024,128]{1,0:T(8,128)(2,1)} %get-tuple-element.63.a_ref) | copy-start | bytes 786436
  167.4 10.3 %copy-start.6 = (bf16[1024,128]{1,0:T(8,128)(2,1)S(1)}, bf16[1024,128]{1,0:T(8,128)(2,1)}, u32[]{:S(2)}) copy-start(bf16[1024,128]{1,0:T(8,128)(2,1)} %get-tuple-element.62.a_ref) | copy-start | bytes 786436
  370.2 20.3 %copy-start.2 = (bf16[4,304,384]{2,1,0:T(8,128)(2,1)S(1)}, bf16[4,304,384]{2,1,0:T(8,128)(2,1)}, u32[]{:S(2)}) copy-start(bf16[4,304,384]{2,1,0:T(8,128)(2,1)} %get-tuple-element.107) | copy-start | bytes 2801668
  390.5 5.6 %collective-permute-start.24 = (f32[8,384]{1,0:T(8,128)}, f32[8,384]{1,0:T(8,128)S(1)}, u32[]{:S(2)}, u32[]{:S(2)}) collective-permute-start(f32[8,384]{1,0:T(8,128)} %dynamic_update_slice.3), channel_id=1, source_target_pairs={{0,8},{8,0},{16,24},{24,16},{1,9},{9,1},{17,25},{25,17},{2,10},{10... | collective-permute-start | bytes 36872 | tf_op jit(solution)/shard_map/ppermute | solution.py:942
  390.6 4.6 copy-start.1
  390.6 74.3 %collective-permute-start.29 = (bf16[304,384]{1,0:T(8,128)(2,1)S(1)}, bf16[304,384]{1,0:T(8,128)(2,1)S(1)}, u32[]{:S(2)}, u32[]{:S(2)}) collective-permute-start(bf16[304,384]{1,0:T(8,128)(2,1)S(1)} %get-tuple-element.117), channel_id=1, source_target_pairs={{24,0},{0,8},{8,16},{16,24},{25,1},{1,9},{9,17},{17,25},{26,2},{2,... | collective-permute-start | bytes 700424 | tf_op jit(solution)/shard_map/ppermute | solution.py:843
  392.7 72.8 %collective-permute-start.30 = (bf16[304,384]{1,0:T(8,128)(2,1)S(1)}, bf16[304,384]{1,0:T(8,128)(2,1)S(1)}, u32[]{:S(2)}, u32[]{:S(2)}) collective-permute-start(bf16[304,384]{1,0:T(8,128)(2,1)S(1)} %get-tuple-element.119), channel_id=1, source_target_pairs={{16,0},{24,8},{0,16},{8,24},{17,1},{25,9},{1,17},{9,25},{18,2},{26... | collective-permute-start | bytes 700424 | tf_op jit(solution)/shard_map/ppermute | solution.py:843
  392.7 72.8 %collective-permute-start.31 = (bf16[304,384]{1,0:T(8,128)(2,1)S(1)}, bf16[304,384]{1,0:T(8,128)(2,1)S(1)}, u32[]{:S(2)}, u32[]{:S(2)}) collective-permute-start(bf16[304,384]{1,0:T(8,128)(2,1)S(1)} %get-tuple-element.118), channel_id=1, source_target_pairs={{8,0},{16,8},{24,16},{0,24},{9,1},{17,9},{25,17},{1,25},{10,2},{18... | collective-permute-start | bytes 700424 | tf_op jit(solution)/shard_map/ppermute | solution.py:843
  395.1 1.0 copy-start.7
  396.1 15.1 %collective-permute-start.25 = (f32[8,384]{1,0:T(8,128)S(1)}, f32[8,384]{1,0:T(8,128)S(1)}, u32[]{:S(2)}, u32[]{:S(2)}) collective-permute-start(f32[8,384]{1,0:T(8,128)S(1)} %add.98), channel_id=1, source_target_pairs={{0,16},{8,24},{16,0},{24,8},{1,17},{9,25},{17,1},{25,9},{2,18},{10... | collective-permute-start | bytes 36872 | tf_op jit(solution)/shard_map/ppermute | solution.py:942
  411.3 13.8 %collective-permute-start.26 = (f32[8,384]{1,0:T(8,128)S(1)}, f32[8,384]{1,0:T(8,128)S(1)}, u32[]{:S(2)}, u32[]{:S(2)}) collective-permute-start(f32[8,384]{1,0:T(8,128)S(1)} %add.99), channel_id=1, source_target_pairs={{0,1},{1,0},{2,3},{3,2},{4,5},{5,4},{6,7},{7,6},{8,9},{9,8},{10,11... | collective-permute-start | bytes 36872 | tf_op jit(solution)/shard_map/ppermute | solution.py:848
  425.1 21.1 %collective-permute-start.27 = (f32[8,384]{1,0:T(8,128)S(1)}, f32[8,384]{1,0:T(8,128)S(1)}, u32[]{:S(2)}, u32[]{:S(2)}) collective-permute-start(f32[8,384]{1,0:T(8,128)S(1)} %add.100), channel_id=1, source_target_pairs={{0,2},{1,3},{2,0},{3,1},{4,6},{5,7},{6,4},{7,5},{8,10},{9,11},{10,... | collective-permute-start | bytes 36872 | tf_op jit(solution)/shard_map/ppermute | solution.py:848
  445.9 19.8 %collective-permute-start.17 = (bf16[304,384]{1,0:T(8,128)(2,1)}, bf16[304,384]{1,0:T(8,128)(2,1)S(1)}, u32[]{:S(2)}, u32[]{:S(2)}) collective-permute-start(bf16[304,384]{1,0:T(8,128)(2,1)} %get-tuple-element.102), channel_id=1, source_target_pairs={{8,0},{16,8},{24,16},{0,24},{9,1},{17,9},{25,17},{1,25},{10,2},{18... | collective-permute-start | bytes 700424 | tf_op jit(solution)/shard_map/ppermute | solution.py:843
  446.3 15.4 %collective-permute-start.28 = (f32[8,384]{1,0:T(8,128)S(1)}, f32[8,384]{1,0:T(8,128)S(1)}, u32[]{:S(2)}, u32[]{:S(2)}) collective-permute-start(f32[8,384]{1,0:T(8,128)S(1)} %add.101), channel_id=1, source_target_pairs={{0,4},{1,5},{2,6},{3,7},{4,0},{5,1},{6,2},{7,3},{8,12},{9,13},{10,... | collective-permute-start | bytes 36872 | tf_op jit(solution)/shard_map/ppermute | solution.py:848
  447.9 13.8 %copy-start.10 = (bf16[304,384]{1,0:T(8,128)(2,1)S(1)}, bf16[304,384]{1,0:T(8,128)(2,1)}, u32[]{:S(2)}) copy-start(bf16[304,384]{1,0:T(8,128)(2,1)} %get-tuple-element.101) | copy-start | bytes 700420
  447.9 17.0 %copy-start.9 = (bf16[304,384]{1,0:T(8,128)(2,1)S(1)}, bf16[304,384]{1,0:T(8,128)(2,1)}, u32[]{:S(2)}) copy-start(bf16[304,384]{1,0:T(8,128)(2,1)} %get-tuple-element.100) | copy-start | bytes 700420
  461.6 18.1 %collective-permute-start.16 = (bf16[304,384]{1,0:T(8,128)(2,1)S(1)}, bf16[304,384]{1,0:T(8,128)(2,1)S(1)}, u32[]{:S(2)}, u32[]{:S(2)}) collective-permute-start(bf16[304,384]{1,0:T(8,128)(2,1)S(1)} %copy-done.10), channel_id=1, source_target_pairs={{16,0},{24,8},{0,16},{8,24},{17,1},{25,9},{1,17},{9,25},{18,2},{26... | collective-permute-start | bytes 700424 | tf_op jit(solution)/shard_map/ppermute | solution.py:843
  464.9 14.8 %collective-permute-start.15 = (bf16[304,384]{1,0:T(8,128)(2,1)S(1)}, bf16[304,384]{1,0:T(8,128)(2,1)S(1)}, u32[]{:S(2)}, u32[]{:S(2)}) collective-permute-start(bf16[304,384]{1,0:T(8,128)(2,1)S(1)} %copy-done.9), channel_id=1, source_target_pairs={{24,0},{0,8},{8,16},{16,24},{25,1},{1,9},{9,17},{17,25},{26,2},{2,... | collective-permute-start | bytes 700424 | tf_op jit(solution)/shard_map/ppermute | solution.py:843
  465.6 15.2 %collective-permute-start.32 = (bf16[304,384]{1,0:T(8,128)(2,1)S(1)}, bf16[304,384]{1,0:T(8,128)(2,1)S(1)}, u32[]{:S(2)}, u32[]{:S(2)}) collective-permute-start(bf16[304,384]{1,0:T(8,128)(2,1)S(1)} %fusion.4), channel_id=1, source_target_pairs={{0,1},{1,0},{2,3},{3,2},{4,5},{5,4},{6,7},{7,6},{8,9},{9,8},{10,11... | collective-permute-start | bytes 700424 | tf_op jit(solution)/shard_map/ppermute | solution.py:848
  480.8 1.6 collective-permute-start.18
  480.9 8.6 %collective-permute-start.33 = (bf16[304,384]{1,0:T(8,128)(2,1)S(1)}, bf16[304,384]{1,0:T(8,128)(2,1)S(1)}, u32[]{:S(2)}, u32[]{:S(2)}) collective-permute-start(bf16[304,384]{1,0:T(8,128)(2,1)S(1)} %add_convert_fusion.1), channel_id=1, source_target_pairs={{0,2},{1,3},{2,0},{3,1},{4,6},{5,7},{6,4},{7,5},{8,10},{9,11},{10,... | collective-permute-start | bytes 700424 | tf_op jit(solution)/shard_map/ppermute | solution.py:848
  482.4 11.7 %collective-permute-start.19 = (bf16[304,384]{1,0:T(8,128)(2,1)S(1)}, bf16[304,384]{1,0:T(8,128)(2,1)S(1)}, u32[]{:S(2)}, u32[]{:S(2)}) collective-permute-start(bf16[304,384]{1,0:T(8,128)(2,1)S(1)} %add_convert_fusion.3), channel_id=1, source_target_pairs={{0,2},{1,3},{2,0},{3,1},{4,6},{5,7},{6,4},{7,5},{8,10},{9,11},{10,... | collective-permute-start | bytes 700424 | tf_op jit(solution)/shard_map/ppermute | solution.py:848
  489.6 7.0 %collective-permute-start.34 = (bf16[304,384]{1,0:T(8,128)(2,1)S(1)}, bf16[304,384]{1,0:T(8,128)(2,1)S(1)}, u32[]{:S(2)}, u32[]{:S(2)}) collective-permute-start(bf16[304,384]{1,0:T(8,128)(2,1)S(1)} %add_convert_fusion), channel_id=1, source_target_pairs={{0,4},{1,5},{2,6},{3,7},{4,0},{5,1},{6,2},{7,3},{8,12},{9,13},{10,... | collective-permute-start | bytes 700424 | tf_op jit(solution)/shard_map/ppermute | solution.py:848
  494.2 7.4 %collective-permute-start.20 = (bf16[304,384]{1,0:T(8,128)(2,1)S(1)}, bf16[304,384]{1,0:T(8,128)(2,1)S(1)}, u32[]{:S(2)}, u32[]{:S(2)}) collective-permute-start(bf16[304,384]{1,0:T(8,128)(2,1)S(1)} %add_convert_fusion.2), channel_id=1, source_target_pairs={{0,4},{1,5},{2,6},{3,7},{4,0},{5,1},{6,2},{7,3},{8,12},{9,13},{10,... | collective-permute-start | bytes 700424 | tf_op jit(solution)/shard_map/ppermute | solution.py:848
  497.6 6.7 %collective-permute-start.21 = (bf16[112,384]{1,0:T(8,128)(2,1)S(1)}, bf16[112,384]{1,0:T(8,128)(2,1)S(1)}, u32[]{:S(2)}, u32[]{:S(2)}) collective-permute-start(bf16[112,384]{1,0:T(8,128)(2,1)S(1)} %get-tuple-element.124), channel_id=1, source_target_pairs={{24,0},{0,8},{8,16},{16,24},{25,1},{1,9},{9,17},{17,25},{26,2},{2,... | collective-permute-start | bytes 258056 | tf_op jit(solution)/shard_map/ppermute | solution.py:843
  497.7 8.4 %collective-permute-start.22 = (bf16[112,384]{1,0:T(8,128)(2,1)S(1)}, bf16[112,384]{1,0:T(8,128)(2,1)S(1)}, u32[]{:S(2)}, u32[]{:S(2)}) collective-permute-start(bf16[112,384]{1,0:T(8,128)(2,1)S(1)} %get-tuple-element.126), channel_id=1, source_target_pairs={{16,0},{24,8},{0,16},{8,24},{17,1},{25,9},{1,17},{9,25},{18,2},{26... | collective-permute-start | bytes 258056 | tf_op jit(solution)/shard_map/ppermute | solution.py:843
  498.0 8.1 %collective-permute-start.23 = (bf16[112,384]{1,0:T(8,128)(2,1)S(1)}, bf16[112,384]{1,0:T(8,128)(2,1)S(1)}, u32[]{:S(2)}, u32[]{:S(2)}) collective-permute-start(bf16[112,384]{1,0:T(8,128)(2,1)S(1)} %get-tuple-element.125), channel_id=1, source_target_pairs={{8,0},{16,8},{24,16},{0,24},{9,1},{17,9},{25,17},{1,25},{10,2},{18... | collective-permute-start | bytes 258056 | tf_op jit(solution)/shard_map/ppermute | solution.py:843
Sparse Core Ops, SparseCore 0:
  395.3 43.7 reduce-scatter.1
